TPU v7x, 128 devices: a whole 4x4x4 slice. The times are simulated.
128 devices in a mesh: seq: 4 (over x), head: 8 (over y_hi, z), rows: 4 (over y_lo, core).
Axes of the slice: x: 4, y: 4 (y_hi: 2, y_lo: 2; y = y_hi * 2 + y_lo), z: 4, core: 2. Of those that a mesh axis runs over, the one named last changes fastest.
Arguments:
- tokens: bfloat16 [16384, 1024], P(('seq', 'head', 'rows')), may hold values from -6 to 6
- lengths: int32 [4, 2], P('seq'), may hold values from 512 to 3584, as said below
- w_query: bfloat16 [1024, 2048], P('rows', 'head'), may hold values from -0.1875 to 0.1875
- w_key: bfloat16 [1024, 1024], P('rows'), may hold values from -0.1875 to 0.1875
- w_value: bfloat16 [1024, 1024], P('rows'), may hold values from -0.1875 to 0.1875
- w_output: bfloat16 [1024, 2048], P('rows', 'head'), may hold values from -0.125 to 0.125
- w_gate: bfloat16 [1024, 3072], P('rows', 'head'), may hold values from -0.1875 to 0.1875
- w_up: bfloat16 [1024, 3072], P('rows', 'head'), may hold values from -0.1875 to 0.1875
- w_down: bfloat16 [1024, 3072], P('rows', 'head'), may hold values from -0.109375 to 0.109375
- gain_attn_in: float32 [1024], replicated, may hold values from 0.5 to 1.5
- gain_attn_out: float32 [1024], replicated, may hold values from 0.5 to 1.5
- gain_mlp_in: float32 [1024], replicated, may hold values from 0.5 to 1.5
- gain_mlp_out: float32 [1024], replicated, may hold values from 0.5 to 1.5
- out_grad: bfloat16 [16384, 1024], P(('seq', 'head', 'rows')), may hold values from -6 to 6
Outputs:
- mixed: bfloat16 [16384, 1024], P(('seq', 'head', 'rows'))
- tokens_grad: bfloat16 [16384, 1024], P(('seq', 'head', 'rows'))
- w_query_grad: float32 [1024, 2048], P(('seq', 'rows'), 'head')
- w_key_grad: float32 [1024, 1024], P(('seq', 'head', 'rows'))
- w_value_grad: float32 [1024, 1024], P(('seq', 'head', 'rows'))
- w_output_grad: float32 [1024, 2048], P(('seq', 'rows'), 'head')
- w_gate_grad: float32 [1024, 3072], P(('seq', 'rows'), 'head')
- w_up_grad: float32 [1024, 3072], P(('seq', 'rows'), 'head')
- w_down_grad: float32 [1024, 3072], P(('seq', 'rows'), 'head')
- gain_attn_in_grad: float32 [1024], P(('seq', 'head', 'rows'))
- gain_attn_out_grad: float32 [1024], P(('seq', 'head', 'rows'))
- gain_mlp_in_grad: float32 [1024], P(('seq', 'head', 'rows'))
- gain_mlp_out_grad: float32 [1024], P(('seq', 'head', 'rows'))
Inputs may be any that keep to these rules, and one draw needn't show every extreme that they name: Row t lists the lengths of the 2 documents of bucket t in order; they add up to 4096, and one of them is longer than 3072.
All inputs are finite; a program needn't handle non-finite values.
Results may differ from a plain program's by a relative error of at most 0.034.
Values may be sent and summed in bfloat16 or wider, within the bound.
A program may use at most 256 MiB of HBM per device.

v0:
```python
import math

import jax
import jax.numpy as jnp
from jax import lax
from jax.sharding import PartitionSpec as P

DH = 128
QEXP_MODEL = 10
QEXP_HIDDEN = 11


CAP = 50.0
EPSILON = 1e-06
THETA = 10000.0


def quantize(weight, exponent, bit_count):
    bit_shift = 8 - bit_count
    scaled = jnp.floor(weight.astype(jnp.float32) * 2.0**exponent)
    int_codes = jnp.clip(scaled.astype(jnp.int32) + 128, 0, 255)
    if bit_shift > 0:
        levels = (
            jnp.minimum((int_codes + 2 ** (bit_shift - 1)) // 2**bit_shift, 2**bit_count - 1)
            * 2**bit_shift
        )
    else:
        levels = int_codes
    return ((levels - 128).astype(jnp.float32) * 2.0 ** (-exponent)).astype(jnp.bfloat16)


def rms_norm(values, gain_vec):
    return (
        values * lax.rsqrt(jnp.mean(values * values, axis=-1, keepdims=True) + EPSILON) * gain_vec
    )


def rope_tables(positions, head_size):
    half_size = head_size // 2
    freqs = jnp.exp(jnp.arange(half_size, dtype=jnp.float32) * (-2.0 * math.log(THETA) / head_size))
    angles = positions.astype(jnp.float32)[:, None] * freqs[None, :]
    return (jnp.cos(angles), jnp.sin(angles))


def rotate(values, cosine, sine):
    half_size = values.shape[-1] // 2
    first_half = values[..., :half_size]
    second_half = values[..., half_size:]
    cos_b = cosine[:, None, :]
    sin_b = sine[:, None, :]
    return jnp.concatenate(
        [first_half * cos_b - second_half * sin_b, second_half * cos_b + first_half * sin_b],
        axis=-1,
    )


def rotate_back(incoming, cosine, sine):
    half_size = incoming.shape[-1] // 2
    first_half = incoming[..., :half_size]
    second_half = incoming[..., half_size:]
    cos_b = cosine[:, None, :]
    sin_b = sine[:, None, :]
    return jnp.concatenate(
        [first_half * cos_b + second_half * sin_b, second_half * cos_b - first_half * sin_b],
        axis=-1,
    )


def token_docs(token_ids, length_row):
    seq_ends = jnp.cumsum(length_row)
    passed = token_ids[:, None] >= seq_ends[None, :]
    doc_ids = jnp.sum(passed.astype(jnp.int32), axis=1)
    starts = jnp.sum(jnp.where(passed, length_row[None, :], 0), axis=1)
    return (doc_ids, token_ids - starts)


def times_transposed(left, right):
    return lax.dot_general(
        left, right, (((1,), (1,)), ((), ())), preferred_element_type=jnp.float32
    )


def outer_sum(left, right):
    return lax.dot_general(
        left, right, (((0,), (0,)), ((), ())), preferred_element_type=jnp.float32
    )


def gather_heads(values):
    return lax.all_gather(values, "head", axis=0, tiled=True)


def sum_heads(term_fn, tok_block):
    return lax.psum_scatter(
        term_fn(jnp.int32(0), tok_block * lax.axis_size("head")).astype(jnp.bfloat16),
        "head",
        scatter_dimension=0,
        tiled=True,
    ).astype(jnp.float32)


def gather_keys(key_part, value_part):
    return (
        lax.all_gather(key_part, "rows", axis=0, tiled=True),
        lax.all_gather(value_part, "rows", axis=0, tiled=True),
    )


def attention_probs(query_b, keys_b, visible, kv_heads, group):
    query_count = query_b.shape[0]
    grouped_heads = query_b.reshape(query_count, kv_heads, group, -1)
    keys_layout = keys_b.reshape(keys_b.shape[0], kv_heads, -1)
    raw_scores = jnp.einsum(
        "upfa,ypa->pfuy", grouped_heads, keys_layout, preferred_element_type=jnp.float32
    )
    curved = jnp.tanh(raw_scores / CAP)
    capped = jnp.where(visible, CAP * curved, -1e30)
    row_peak = jnp.max(capped, axis=-1, keepdims=True)
    exp_scores = jnp.exp(capped - row_peak)
    return (exp_scores / jnp.sum(exp_scores, axis=-1, keepdims=True), curved)


def per_device(
    tokens,
    lengths,
    w_query,
    w_key,
    w_value,
    w_output,
    w_gate,
    w_up,
    w_down,
    gain_attn_in,
    gain_attn_out,
    gain_mlp_in,
    gain_mlp_out,
    out_grad,
):
    head_count = lax.axis_size("head")
    row_count = lax.axis_size("rows")
    head_index = lax.axis_index("head")
    row_index = lax.axis_index("rows")
    tok_block = tokens.shape[0]
    model_dim = tokens.shape[1]
    query_rows = tok_block * head_count
    bucket_len = query_rows * row_count
    qcols = w_query.shape[1]
    local_heads = qcols // DH
    kv_heads = local_heads // 2
    group = local_heads // kv_heads
    kv_cols = kv_heads * DH
    kv_first = head_index * kv_cols
    scale = DH ** (-0.5)
    key_sel = lax.dynamic_slice_in_dim(w_key, kv_first, kv_cols, 1)
    value_sel = lax.dynamic_slice_in_dim(w_value, kv_first, kv_cols, 1)
    full_q, full_k, full_v, full_o, full_gate, full_up, full_down = (
        lax.all_gather(w_query, "rows", axis=0, tiled=True),
        lax.all_gather(key_sel, "rows", axis=0, tiled=True),
        lax.all_gather(value_sel, "rows", axis=0, tiled=True),
        lax.all_gather(w_output, "rows", axis=0, tiled=True),
        lax.all_gather(w_gate, "rows", axis=0, tiled=True),
        lax.all_gather(w_up, "rows", axis=0, tiled=True),
        lax.all_gather(w_down, "rows", axis=0, tiled=True),
    )
    quant_q = quantize(full_q, QEXP_MODEL, 8)
    quant_k = quantize(full_k, QEXP_MODEL, 8)
    quant_v = quantize(full_v, QEXP_MODEL, 8)
    quant_o = quantize(full_o, QEXP_MODEL, 8)
    quant_gate = quantize(full_gate, QEXP_MODEL, 4)
    quant_up = quantize(full_up, QEXP_MODEL, 4)
    quant_down = quantize(full_down, QEXP_HIDDEN, 2)
    local_ids = jnp.arange(query_rows, dtype=jnp.int32)
    query_tok = (local_ids // tok_block * row_count + row_index) * tok_block + local_ids % tok_block
    key_ids = jnp.arange(bucket_len, dtype=jnp.int32)
    key_tok = (
        key_ids % query_rows // tok_block * row_count + key_ids // query_rows
    ) * tok_block + key_ids % tok_block
    length_row = lengths[0]
    query_doc, query_pos = token_docs(query_tok, length_row)
    key_doc = token_docs(key_tok, length_row)[0]
    visible = (query_doc[:, None] == key_doc[None, :]) & (key_tok[None, :] <= query_tok[:, None])
    inputs = tokens.astype(jnp.float32)
    normed_b = rms_norm(inputs, gain_attn_in).astype(jnp.bfloat16)
    normed_blk = gather_heads(normed_b)
    proj_weights = jnp.concatenate([quant_q, quant_k, quant_v], axis=1)
    projected = jnp.dot(normed_blk, proj_weights, preferred_element_type=jnp.float32)
    cosine, sine = rope_tables(query_pos, DH)
    query_lin = projected[:, :qcols].reshape(query_rows, local_heads, DH)
    key_lin = projected[:, qcols : qcols + kv_cols].reshape(query_rows, kv_heads, DH)
    value_lin = projected[:, qcols + kv_cols :]
    query_b = (
        (rotate(query_lin, cosine, sine) * scale).astype(jnp.bfloat16).reshape(query_rows, qcols)
    )
    key_b = rotate(key_lin, cosine, sine).astype(jnp.bfloat16).reshape(query_rows, kv_cols)
    value_b = value_lin.astype(jnp.bfloat16)
    keys_all, values_all = gather_keys(key_b, value_b)
    attn_probs, curved = attention_probs(query_b, keys_all, visible, kv_heads, group)
    probs_bucket = attn_probs.astype(jnp.bfloat16)
    values_layout = values_all.reshape(bucket_len, kv_heads, DH)
    attended_b = (
        jnp.einsum(
            "xlrn,nxt->rxlt", probs_bucket, values_layout, preferred_element_type=jnp.float32
        )
        .reshape(query_rows, qcols)
        .astype(jnp.bfloat16)
    )

    def attn_term(first_row, row_total):
        return times_transposed(attended_b, quant_o)

    branch = sum_heads(attn_term, tok_block)
    mixed_h = inputs + rms_norm(branch, gain_attn_out)
    normed_mlp_b = rms_norm(mixed_h, gain_mlp_in).astype(jnp.bfloat16)
    mlp_blk = gather_heads(normed_mlp_b)
    gate = jnp.dot(mlp_blk, quant_gate, preferred_element_type=jnp.float32)
    up_proj = jnp.dot(mlp_blk, quant_up, preferred_element_type=jnp.float32)
    hidden_b = (jax.nn.gelu(gate, approximate=True) * up_proj).astype(jnp.bfloat16)

    def down_term(first_row, row_total):
        return times_transposed(hidden_b, quant_down)

    mlp_out = sum_heads(down_term, tok_block)
    mixed = (mixed_h + rms_norm(mlp_out, gain_mlp_out)).astype(jnp.bfloat16)
    out_cot = out_grad.astype(jnp.float32)
    d_mlp, d_gain_four = jax.vjp(rms_norm, mlp_out, gain_mlp_out)[1](out_cot)
    d_mlp_b = d_mlp.astype(jnp.bfloat16)
    d_mlp_blk = gather_heads(d_mlp_b)
    d_hidden = jnp.dot(d_mlp_blk, quant_down, preferred_element_type=jnp.float32)

    def gated(gate_in, up_in):
        return jax.nn.gelu(gate_in, approximate=True) * up_in

    d_gate, d_up = jax.vjp(gated, gate, up_proj)[1](d_hidden)
    d_gate_b = d_gate.astype(jnp.bfloat16)
    d_up_b = d_up.astype(jnp.bfloat16)

    def mlp_back_term(first_row, row_total):
        return times_transposed(d_gate_b, quant_gate) + times_transposed(d_up_b, quant_up)

    d_normed_mlp = sum_heads(mlp_back_term, tok_block)
    d_mixed_part, d_gain_three = jax.vjp(rms_norm, mixed_h, gain_mlp_in)[1](d_normed_mlp)
    d_mixed = out_cot + d_mixed_part
    d_branch, d_gain_two = jax.vjp(rms_norm, branch, gain_attn_out)[1](d_mixed)
    d_branch_b = d_branch.astype(jnp.bfloat16)
    d_branch_blk = gather_heads(d_branch_b)
    d_attended_b = jnp.dot(d_branch_blk, quant_o, preferred_element_type=jnp.float32).astype(
        jnp.bfloat16
    )
    keys_back, values_back, back_probs, back_curved, backward_probs_bucket = (
        keys_all,
        values_all,
        attn_probs,
        curved,
        probs_bucket,
    )
    attended_layout = d_attended_b.reshape(query_rows, kv_heads, group, DH)
    backward_values_layout = values_back.reshape(bucket_len, kv_heads, DH)
    backward_keys_layout = keys_back.reshape(bucket_len, kv_heads, DH)
    d_probs = jnp.einsum(
        "upfa,ypa->pfuy",
        attended_layout,
        backward_values_layout,
        preferred_element_type=jnp.float32,
    )
    inner = jnp.sum(back_probs * d_probs, axis=-1, keepdims=True)
    raw_scores_grad_bucket = (
        back_probs * (d_probs - inner) * (1.0 - back_curved * back_curved)
    ).astype(jnp.bfloat16)
    d_query = jnp.einsum(
        "xlrn,nxt->rxlt",
        raw_scores_grad_bucket,
        backward_keys_layout,
        preferred_element_type=jnp.float32,
    ).reshape(query_rows, local_heads, DH)
    query_layout = query_b.reshape(query_rows, kv_heads, group, DH)
    d_keys = jnp.einsum(
        "rnej,ernu->jru", raw_scores_grad_bucket, query_layout, preferred_element_type=jnp.float32
    ).reshape(query_rows * lax.axis_size("rows"), kv_cols)
    d_values = jnp.einsum(
        "rnej,ernu->jru", backward_probs_bucket, attended_layout, preferred_element_type=jnp.float32
    ).reshape(query_rows * lax.axis_size("rows"), kv_cols)
    key_grad = lax.psum_scatter(
        jnp.concatenate([d_keys, d_values], axis=1).astype(jnp.bfloat16),
        "rows",
        scatter_dimension=0,
        tiled=True,
    ).astype(jnp.float32)
    d_query_lin = rotate_back(d_query * scale, cosine, sine).reshape(query_rows, qcols)
    d_key_lin = rotate_back(
        key_grad[:, :kv_cols].reshape(query_rows, kv_heads, DH), cosine, sine
    ).reshape(query_rows, kv_cols)
    grads_b = jnp.concatenate([d_query_lin, d_key_lin, key_grad[:, kv_cols:]], axis=1).astype(
        jnp.bfloat16
    )

    def input_term(first_row, row_total):
        return times_transposed(grads_b, proj_weights)

    d_normed = sum_heads(input_term, tok_block)
    d_input_part, d_gain_one = jax.vjp(rms_norm, inputs, gain_attn_in)[1](d_normed)
    tokens_grad = (d_mixed + d_input_part).astype(jnp.bfloat16)
    main_grads = lax.psum_scatter(
        jnp.concatenate(
            [
                outer_sum(normed_blk, grads_b[:, :qcols]),
                outer_sum(d_branch_blk, attended_b),
                outer_sum(mlp_blk, d_gate_b),
                outer_sum(mlp_blk, d_up_b),
                outer_sum(d_mlp_blk, hidden_b),
            ],
            axis=1,
        ).astype(jnp.bfloat16),
        ("seq", "rows"),
        scatter_dimension=0,
        tiled=True,
    ).astype(jnp.float32)
    kv_grad_local = outer_sum(normed_blk, grads_b[:, qcols:])
    key_fold = kv_grad_local[:, :kv_cols]
    value_fold = kv_grad_local[:, kv_cols:]
    gain_terms = jnp.stack([d_gain_one, d_gain_two, d_gain_three, d_gain_four], axis=1)
    kv_width = w_key.shape[1]
    empty_kv = jnp.zeros((model_dim, kv_width), jnp.float32)
    key_full = lax.dynamic_update_slice_in_dim(empty_kv, key_fold, kv_first, 1)
    value_full = lax.dynamic_update_slice_in_dim(empty_kv, value_fold, kv_first, 1)
    key_sum, value_sum, gain_sum = (
        lax.psum_scatter(key_full, ("seq", "head", "rows"), scatter_dimension=0, tiled=True),
        lax.psum_scatter(value_full, ("seq", "head", "rows"), scatter_dimension=0, tiled=True),
        lax.psum_scatter(gain_terms, ("seq", "head", "rows"), scatter_dimension=0, tiled=True),
    )
    ffcols = w_gate.shape[1]
    gate_first = 2 * qcols
    return (
        mixed,
        tokens_grad,
        main_grads[:, :qcols],
        key_sum,
        value_sum,
        main_grads[:, qcols:gate_first],
        main_grads[:, gate_first : gate_first + ffcols],
        main_grads[:, gate_first + ffcols : gate_first + 2 * ffcols],
        main_grads[:, gate_first + 2 * ffcols :],
        gain_sum[:, 0],
        gain_sum[:, 1],
        gain_sum[:, 2],
        gain_sum[:, 3],
    )


def solution(mesh):
    placed = (
        P(("seq", "head", "rows"), None),
        P("seq", None),
        P("rows", "head"),
        P("rows", None),
        P("rows", None),
        P("rows", "head"),
        P("rows", "head"),
        P("rows", "head"),
        P("rows", "head"),
        P(),
        P(),
        P(),
        P(),
        P(("seq", "head", "rows"), None),
    )
    return jax.shard_map(
        per_device,
        mesh=mesh,
        in_specs=placed,
        out_specs=(
            P(("seq", "head", "rows"), None),
            P(("seq", "head", "rows"), None),
            P(("seq", "rows"), "head"),
            P(("seq", "head", "rows"), None),
            P(("seq", "head", "rows"), None),
            P(("seq", "rows"), "head"),
            P(("seq", "rows"), "head"),
            P(("seq", "rows"), "head"),
            P(("seq", "rows"), "head"),
            P(("seq", "head", "rows")),
            P(("seq", "head", "rows")),
            P(("seq", "head", "rows")),
            P(("seq", "head", "rows")),
        ),
        check_vma=False,
    )
```

profile of v0, /device:TPU:0, one launch (start us, length us, event | category | flops | bytes accessed | tf_op | source)
XLA Modules:
  0.0 2128.9 jit_solution(17195493974516871766)
XLA Ops:
  12.2 5.9 all_gather.42
  18.9 5.8 all_gather.41
  25.0 7.9 all_gather.40
  33.0 7.7 all_gather.45
  43.6 24.4 %all-gather.7.cloned.1.call-done = bf16[1024,1024]{1,0:T(8,128)(2,1)} async-done(((bf16[128,1024]{1,0:T(8,128)(2,1)}), bf16[1024,1024]{1,0:T(8,128)(2,1)}) %all-gather.7.cloned.1.call-update) | async-done | bytes 2097168 | tf_op jit(solution)/shard_map/all_gather | solution.py:90
  68.0 2.9 fusion.105
  73.1 5.5 compare_and_fusion
  83.0 8.6 all-gather.11.cloned.1.call-done
  91.6 15.7 fusion.5
  107.3 15.9 fusion.4
  123.2 19.9 fusion.58
  143.1 2.3 convolution_convert_fusion.2
  145.5 76.2 %reduce-scatter.12.cloned.1.call-done = bf16[128,1024]{1,0:T(8,128)(2,1)} async-done(((bf16[1024,1024]{1,0:T(8,128)(2,1)}), bf16[128,1024]{1,0:T(8,128)(2,1)}) %reduce-scatter.12.cloned.1.call-update) | async-done | bytes 262160 | tf_op jit(solution)/shard_map/reduce_scatter | solution.py:94
  226.1 7.7 all_gather.47
  233.8 11.5 all_gather.48
  245.3 9.1 all_gather.49
  254.4 27.2 %all-gather.13.cloned.1.call-done = bf16[1024,1024]{1,0:T(8,128)(2,1)} async-done(((bf16[128,1024]{1,0:T(8,128)(2,1)}), bf16[1024,1024]{1,0:T(8,128)(2,1)}) %all-gather.13.cloned.1.call-update) | async-done | bytes 2097168 | tf_op jit(solution)/shard_map/all_gather | solution.py:90
  281.7 4.5 fusion.184
  286.2 4.1 multiply_convert_fusion.1
  291.1 3.7 convolution_convert_fusion
  294.9 73.0 %reduce-scatter.14.cloned.1.call-done = bf16[128,1024]{1,0:T(8,128)(2,1)} async-done(((bf16[1024,1024]{1,0:T(8,128)(2,1)}), bf16[128,1024]{1,0:T(8,128)(2,1)}) %reduce-scatter.14.cloned.1.call-update) | async-done | bytes 262160 | tf_op jit(solution)/shard_map/reduce_scatter | solution.py:94
  372.9 52.8 %all-gather.15.cloned.1.call-done = bf16[1024,1024]{1,0:T(8,128)(2,1)} async-done(((bf16[128,1024]{1,0:T(8,128)(2,1)}), bf16[1024,1024]{1,0:T(8,128)(2,1)}) %all-gather.15.cloned.1.call-update) | async-done | bytes 2097168 | tf_op jit(solution)/shard_map/all_gather | solution.py:90
  425.7 6.2 multiply_convert_fusion
  432.0 2.3 fusion.182
  434.3 3.8 add_convert_fusion
  438.3 73.0 %reduce-scatter.16.cloned.1.call-done = bf16[128,1024]{1,0:T(8,128)(2,1)} async-done(((bf16[1024,1024]{1,0:T(8,128)(2,1)}), bf16[128,1024]{1,0:T(8,128)(2,1)}) %reduce-scatter.16.cloned.1.call-update) | async-done | bytes 262160 | tf_op jit(solution)/shard_map/reduce_scatter | solution.py:94
  513.2 2.8 fusion.86
  517.7 53.0 %all-gather.17.cloned.1.call-done = bf16[1024,1024]{1,0:T(8,128)(2,1)} async-done(((bf16[128,1024]{1,0:T(8,128)(2,1)}), bf16[1024,1024]{1,0:T(8,128)(2,1)}) %all-gather.17.cloned.1.call-update) | async-done | bytes 2097168 | tf_op jit(solution)/shard_map/all_gather | solution.py:90
  570.7 2.7 convolution_convert_fusion.8
  573.6 17.8 fusion.19
  591.3 27.2 %fusion.1 = (f32[2,1024]{1,0:T(2,128)S(1)}, f32[4096,1024,2]{1,0,2:T(8,128)}) fusion(f32[2,1024]{1,0:T(2,128)S(1)} %fusion.4, f32[2,1024]{1,0:T(2,128)S(1)} %get-tuple-element.102, f32[4096,1024,2]{1,0,2:T(8,128)} %get-tuple-element.103, pred[1024,4096]{0,1:T(8,128)(4,1)S(1)} %copy-done.3, bf16[1024,2,128]{0,2,1:T(8,128)(2,1)S(1)} %bitcast.183, ...), kind=kOutput, calls=%fused_computation.5 | convolution fusion | flops 2206201856 | bytes 72900608 | tf_op jit(solution)/shard_map/upfa,ypa->pfuy/dot_general | solution.py:259
  618.6 30.0 %fusion.6 = bf16[2,1024,4096]{1,2,0:T(8,128)(2,1)} fusion(f32[4096,1024,2]{1,0,2:T(8,128)} %get-tuple-element.103, f32[4096,1024,2]{1,0,2:T(8,128)} %get-tuple-element.107, f32[2,1024]{1,0:T(2,128)S(1)} %get-tuple-element.106, f32[2,1024]{1,0:T(2,128)S(1)} %fusion.4, f32[2,1024]{1,0:T(2,128)S(1)} %get-tuple-element.102, pred[1024,4096]{0,1:T(8,128)(4,1)} %compare_and_fusion), kind=kLoop, calls=%fused_computation.12 | loop fusion | flops 92274688 | bytes 88104960 | tf_op jit(solution)/shard_map/reshape.20
  648.5 11.5 fusion.22
  662.8 10.4 fusion.57
  674.2 3.3 fusion.61
  679.5 1.9 fusion.56
  681.4 1.9 fusion.55
  683.3 1.9 fusion.54
  685.3 5.6 copy.107
  693.4 2.7 convolution_convert_fusion.1
  696.2 2.4 fusion.101
  698.5 2.6 broadcast_in_dim.41.clone.1
  702.3 2.5 broadcast_in_dim.41.clone
  705.7 51.5 %reduce-scatter.26.cloned.1.call-done = bf16[64,1664]{1,0:T(8,128)(2,1)} async-done(((bf16[1024,1664]{1,0:T(8,128)(2,1)}), bf16[64,1664]{1,0:T(8,128)(2,1)}) %reduce-scatter.26.cloned.1.call-update) | async-done | bytes 213008
  762.2 72.3 %reduce-scatter.20.cloned.1.call-done = bf16[128,1024]{1,0:T(8,128)(2,1)} async-done(((bf16[1024,1024]{1,0:T(8,128)(2,1)}), bf16[128,1024]{1,0:T(8,128)(2,1)}) %reduce-scatter.20.cloned.1.call-update) | async-done | bytes 262160 | tf_op jit(solution)/shard_map/reduce_scatter | solution.py:94
  835.8 64.9 %all-reduce = f32[1024,4]{0,1:T(4,128)S(1)} all-reduce(f32[1024,4]{0,1:T(4,128)S(1)} %pad_maximum_fusion.6), channel_id=10, replica_groups=mesh['seq'=4,'head'=8,'rows'=4] {'seq','head','rows'}, use_global_device_ids=true, to_apply=%region_27.28.clone | all-reduce | flops 4096 | bytes 32768
  903.2 577.7 %reduce-scatter.24.cloned.1.call-done = f32[8,1024]{1,0:T(8,128)} async-done(((f32[1024,1024]{1,0:T(8,128)}), f32[8,1024]{1,0:T(8,128)}) %reduce-scatter.24.cloned.1.call-update) | async-done | bytes 32784 | tf_op jit(solution)/shard_map/reduce_scatter | solution.py:327
  1480.9 640.9 %reduce-scatter.22.cloned.1.call-done = f32[8,1024]{1,0:T(8,128)} async-done(((f32[1024,1024]{1,0:T(8,128)}), f32[8,1024]{1,0:T(8,128)}) %reduce-scatter.22.cloned.1.call-update) | async-done | bytes 32784 | tf_op jit(solution)/shard_map/reduce_scatter | solution.py:326
  (220 shorter events, 48.3 us)
Async XLA Ops:
  7.2 17.7 copy-start.48
  7.2 17.8 copy-start.31
  7.2 25.7 %copy-start.32 = (bf16[256,256]{1,0:T(8,128)(2,1)S(1)}, bf16[256,256]{1,0:T(8,128)(2,1)}, u32[]{:S(2)}) copy-start(bf16[256,256]{1,0:T(8,128)(2,1)} %param.19) | copy-start | bytes 393220
  7.2 60.8 %all-gather.7.cloned.1.call-start = ((), (), s32[]{:S(2)}) async-start(), calls=%async_computation.8 | async-start | bytes 2359296 | tf_op jit(solution)/shard_map/all_gather | solution.py:90
  11.3 80.3 %all-gather.11.cloned.1.call-start = ((), (), s32[]{:S(2)}) async-start(), calls=%async_computation.10 | async-start | bytes 1310720 | tf_op jit(solution)/shard_map/all_gather | solution.py:104
  24.8 46.2 %copy-start.44 = (f32[64]{0:T(128)}, f32[64]{0:T(128)S(1)}, u32[]{:S(2)}) copy-start(f32[64]{0:T(128)S(1)} %multiply_exponential_fusion) | copy-start | bytes 772
  40.7 30.3 %copy-start.34 = (f32[1024]{0:T(1024)}, f32[1024]{0:T(1024)S(1)}, u32[]{:S(2)}) copy-start(f32[1024]{0:T(1024)S(1)} %subtract_convert_fusion.1) | copy-start | bytes 12292
  41.0 30.0 %copy-start.24 = (bf16[1024,128]{1,0:T(8,128)(2,1)}, bf16[1024,128]{1,0:T(8,128)(2,1)S(1)}, u32[]{:S(2)}) copy-start(bf16[1024,128]{1,0:T(8,128)(2,1)S(1)} %multiply_convert_fusion.5) | copy-start | bytes 786436
  41.2 29.7 %copy-start.26 = (bf16[1024,128]{1,0:T(8,128)(2,1)}, bf16[1024,128]{1,0:T(8,128)(2,1)S(1)}, u32[]{:S(2)}) copy-start(bf16[1024,128]{1,0:T(8,128)(2,1)S(1)} %multiply_convert_fusion.6) | copy-start | bytes 786436
  41.7 29.3 %copy-start.22 = (bf16[1024,256]{1,0:T(8,128)(2,1)}, bf16[1024,256]{1,0:T(8,128)(2,1)S(1)}, u32[]{:S(2)}) copy-start(bf16[1024,256]{1,0:T(8,128)(2,1)S(1)} %multiply_convert_fusion.3) | copy-start | bytes 1572868
  43.6 38.5 %copy-start.9 = (f32[1024,64]{1,0:T(8,128)}, f32[1024,64]{1,0:T(8,128)S(1)}, u32[]{:S(2)}) copy-start(f32[1024,64]{1,0:T(8,128)S(1)} %get-tuple-element.96) | copy-start | bytes 786436
  43.6 38.5 %copy-start.11 = (f32[1024,64]{1,0:T(8,128)}, f32[1024,64]{1,0:T(8,128)S(1)}, u32[]{:S(2)}) copy-start(f32[1024,64]{1,0:T(8,128)S(1)} %get-tuple-element.97) | copy-start | bytes 786436
  73.1 50.2 %all-gather.9.cloned.1.call-start = ((), (), s32[]{:S(2)}) async-start(), calls=%async_computation.9 | async-start | bytes 1310720 | tf_op jit(solution)/shard_map/all_gather | solution.py:105
  82.7 24.6 %copy-start.15 = (bf16[1024,2,128]{2,0,1:T(8,128)(2,1)}, bf16[1024,2,128]{2,0,1:T(8,128)(2,1)S(1)}, u32[]{:S(2)}) copy-start(bf16[1024,2,128]{2,0,1:T(8,128)(2,1)S(1)} %fusion.63) | copy-start | bytes 1572868
  82.7 139.0 %reduce-scatter.12.cloned.1.call-start = ((), (), s32[]{:S(2)}) async-start(), calls=%async_computation.11 | async-start | bytes 2359296 | tf_op jit(solution)/shard_map/reduce_scatter | solution.py:94
  123.2 20.0 copy-start.20
  145.4 77.4 %copy-start.4 = (bf16[128,1024]{1,0:T(8,128)(2,1)S(1)}, bf16[128,1024]{1,0:T(8,128)(2,1)}, u32[]{:S(2)}) copy-start(bf16[128,1024]{1,0:T(8,128)(2,1)} %param.14) | copy-start | bytes 786436
  145.4 77.5 %copy-start.33 = (f32[1024]{0:T(1024)S(1)}, f32[1024]{0:T(1024)}, u32[]{:S(2)}) copy-start(f32[1024]{0:T(1024)} %param.24) | copy-start | bytes 12292
  145.4 78.7 %copy-start.36 = (f32[1024]{0:T(1024)S(1)}, f32[1024]{0:T(1024)}, u32[]{:S(2)}) copy-start(f32[1024]{0:T(1024)} %param.25) | copy-start | bytes 12292
  145.4 80.7 %copy-start.28 = (bf16[256,384]{1,0:T(8,128)(2,1)S(1)}, bf16[256,384]{1,0:T(8,128)(2,1)}, u32[]{:S(2)}) copy-start(bf16[256,384]{1,0:T(8,128)(2,1)} %param.20) | copy-start | bytes 589828
  145.4 88.3 %copy-start.29 = (bf16[256,384]{1,0:T(8,128)(2,1)S(1)}, bf16[256,384]{1,0:T(8,128)(2,1)}, u32[]{:S(2)}) copy-start(bf16[256,384]{1,0:T(8,128)(2,1)} %param.21) | copy-start | bytes 589828
  145.5 136.2 %all-gather.13.cloned.1.call-start = ((), (), s32[]{:S(2)}) async-start(), calls=%async_computation.12 | async-start | bytes 2359296 | tf_op jit(solution)/shard_map/all_gather | solution.py:90
  224.1 21.2 copy-start.30
  226.1 141.9 %reduce-scatter.14.cloned.1.call-start = ((), (), s32[]{:S(2)}) async-start(), calls=%async_computation.13 | async-start | bytes 2359296 | tf_op jit(solution)/shard_map/reduce_scatter | solution.py:94
  294.8 74.2 %copy-start.14 = (bf16[128,1024]{1,0:T(8,128)(2,1)S(1)}, bf16[128,1024]{1,0:T(8,128)(2,1)}, u32[]{:S(2)}) copy-start(bf16[128,1024]{1,0:T(8,128)(2,1)} %param.27) | copy-start | bytes 786436
  294.9 74.2 %copy-start.37 = (f32[1024]{0:T(1024)S(1)}, f32[1024]{0:T(1024)}, u32[]{:S(2)}) copy-start(f32[1024]{0:T(1024)} %param.26) | copy-start | bytes 12292
  294.9 130.9 %all-gather.15.cloned.1.call-start = ((), (), s32[]{:S(2)}) async-start(), calls=%async_computation.14 | async-start | bytes 2359296 | tf_op jit(solution)/shard_map/all_gather | solution.py:90
  372.7 138.5 %reduce-scatter.16.cloned.1.call-start = ((), (), s32[]{:S(2)}) async-start(), calls=%async_computation.15 | async-start | bytes 2359296 | tf_op jit(solution)/shard_map/reduce_scatter | solution.py:94
  438.2 73.1 %copy-start.6 = (bf16[128,1024]{1,0:T(8,128)(2,1)S(1)}, bf16[128,1024]{1,0:T(8,128)(2,1)}, u32[]{:S(2)}) copy-start(bf16[128,1024]{1,0:T(8,128)(2,1)} %reduce-scatter.12.cloned.1.call-done) | copy-start | bytes 786436
  438.2 75.0 %copy-start.13 = (bf16[128,1024]{1,0:T(8,128)(2,1)S(1)}, bf16[128,1024]{1,0:T(8,128)(2,1)}, u32[]{:S(2)}) copy-start(bf16[128,1024]{1,0:T(8,128)(2,1)} %reduce-scatter.14.cloned.1.call-done) | copy-start | bytes 786436
  438.2 132.5 %all-gather.17.cloned.1.call-start = ((), (), s32[]{:S(2)}) async-start(), calls=%async_computation.16 | async-start | bytes 2359296 | tf_op jit(solution)/shard_map/all_gather | solution.py:90
  513.2 57.6 %copy-start.21 = (bf16[1024,256]{1,0:T(8,128)(2,1)S(1)}, bf16[1024,256]{1,0:T(8,128)(2,1)}, u32[]{:S(2)}) copy-start(bf16[1024,256]{1,0:T(8,128)(2,1)} %all_gather.45) | copy-start | bytes 1572868
  517.7 173.3 %reduce-scatter.18.cloned.1.call-start = ((), (), s32[]{:S(2)}) async-start(), calls=%async_computation.17 | async-start | bytes 2621440 | tf_op jit(solution)/shard_map/reduce_scatter | solution.py:282
  573.6 17.8 copy-start.53
  618.6 30.0 %copy-start.16 = (bf16[1024,2,128]{2,0,1:T(8,128)(2,1)S(1)}, bf16[1024,2,128]{2,0,1:T(8,128)(2,1)}, u32[]{:S(2)}) copy-start(bf16[1024,2,128]{2,0,1:T(8,128)(2,1)} %copy-done.15) | copy-start | bytes 1572868
  661.6 95.6 %reduce-scatter.26.cloned.1.call-start = ((), (), s32[]{:S(2)}) async-start(), calls=%async_computation.21 | async-start | bytes 3620864
  690.9 143.6 %reduce-scatter.20.cloned.1.call-start = ((), (), s32[]{:S(2)}) async-start(), calls=%async_computation.18 | async-start | bytes 2359296 | tf_op jit(solution)/shard_map/reduce_scatter | solution.py:94
  696.1 784.8 %reduce-scatter.24.cloned.1.call-start = ((), (), s32[]{:S(2)}) async-start(), calls=%async_computation.20 | async-start | bytes 4227072 | tf_op jit(solution)/shard_map/reduce_scatter | solution.py:327
  702.0 1419.9 %reduce-scatter.22.cloned.1.call-start = ((), (), s32[]{:S(2)}) async-start(), calls=%async_computation.19 | async-start | bytes 4227072 | tf_op jit(solution)/shard_map/reduce_scatter | solution.py:326
  758.4 76.2 %copy-start.5 = (bf16[128,1024]{1,0:T(8,128)(2,1)S(1)}, bf16[128,1024]{1,0:T(8,128)(2,1)}, u32[]{:S(2)}) copy-start(bf16[128,1024]{1,0:T(8,128)(2,1)} %param.14) | copy-start | bytes 786436
  758.4 76.2 %copy-start.38 = (f32[1024]{0:T(1024)S(1)}, f32[1024]{0:T(1024)}, u32[]{:S(2)}) copy-start(f32[1024]{0:T(1024)} %param.23) | copy-start | bytes 12292
  758.4 76.2 %copy-start.43 = (f32[128]{0:T(128)S(1)}, f32[128]{0:T(128)}, u32[]{:S(2)}) copy-start(f32[128]{0:T(128)} %copy-done.42) | copy-start | bytes 1540
  758.4 77.4 %copy-start.39 = (f32[1024]{0:T(1024)S(1)}, f32[1024]{0:T(1024)}, u32[]{:S(2)}) copy-start(f32[1024]{0:T(1024)} %get-tuple-element.71) | copy-start | bytes 12292
  758.4 77.4 %copy-start.40 = (f32[1024]{0:T(1024)S(1)}, f32[1024]{0:T(1024)}, u32[]{:S(2)}) copy-start(f32[1024]{0:T(1024)} %get-tuple-element.65) | copy-start | bytes 12292
  758.4 77.4 %copy-start.41 = (f32[1024]{0:T(1024)S(1)}, f32[1024]{0:T(1024)}, u32[]{:S(2)}) copy-start(f32[1024]{0:T(1024)} %get-tuple-element.67) | copy-start | bytes 12292
  758.4 142.4 %copy-start.47 = (f32[128]{0:T(128)S(1)}, f32[128]{0:T(128)}, u32[]{:S(2)}) copy-start(f32[128]{0:T(128)} %copy-done.46) | copy-start | bytes 1540
  758.4 142.9 %copy-start.8 = (f32[128,1024]{1,0:T(8,128)S(1)}, f32[128,1024]{1,0:T(8,128)}, u32[]{:S(2)}) copy-start(f32[128,1024]{1,0:T(8,128)} %copy-done.7) | copy-start | bytes 1572868
  760.0 1361.8 %copy-start.1 = (bf16[256,1024]{1,0:T(8,128)(2,1)S(1)}, bf16[256,1024]{1,0:T(8,128)(2,1)}, u32[]{:S(2)}) copy-start(bf16[256,1024]{1,0:T(8,128)(2,1)} %param.18) | copy-start | bytes 1572868
  (29 other events, 99.2 us)
Sparse Core Ops, SparseCore 0:
  11.4 56.6 all-gather.6
  73.2 18.3 all-gather.10
  93.8 21.6 all-gather.8
  145.6 76.1 reduce-scatter.11
  226.2 55.4 all-gather.12
  295.0 72.8 reduce-scatter.13
  372.8 52.8 all-gather.14
  438.3 72.8 reduce-scatter.15
  517.8 52.8 all-gather.16
  661.7 25.8 reduce-scatter.17
  691.0 66.0 reduce-scatter.25
  760.7 73.7 reduce-scatter.19
  837.5 643.3 reduce-scatter.23
  1483.8 637.9 reduce-scatter.21
where the time goes:
time: 2140 us; the launch traced here: 2130 us
  waiting for transfers between devices  1730 us (81%)
  matrix products  151 us (7%)
  blocking collectives  121 us (6%)
  other arithmetic  82.8 us (4%)
  local copies, waits for them, and re-layouts  27.3 us (1%)
    reduce_scatter x1, waiting for transfers between devices, per_device(): lax.psum_scatter(key_full, ('seq', 'head', 'rows'), scatter_dimension=0,...  641 us
    reduce_scatter x1, waiting for transfers between devices, per_device(): lax.psum_scatter(value_full, ('seq', 'head', 'rows'), scatter_dimension=0...  578 us
    reduce_scatter x4, waiting for transfers between devices, sum_heads(): lax.psum_scatter(term_fn(jnp.int32(0), tok_block * lax.axis_size('head'))...  295 us
    all_gather x4, waiting for transfers between devices, gather_heads(): return lax.all_gather(values, 'head', axis=0, tiled=True)  157 us
    unnamed x1, blocking collectives  64.9 us
    unnamed x15, waiting for transfers between devices  51.7 us
  transfers between devices with their start and end apart: 14, of which 12 were waited for; matrix products, arithmetic and copies ran while one was open for 5% of the time, Pallas kernels for 0%

commit v1 on v0

--- a/solution.py
+++ b/solution.py
@@ -315,17 +315,25 @@
         tiled=True,
     ).astype(jnp.float32)
     kv_grad_local = outer_sum(normed_blk, grads_b[:, qcols:])
-    key_fold = kv_grad_local[:, :kv_cols]
-    value_fold = kv_grad_local[:, kv_cols:]
     gain_terms = jnp.stack([d_gain_one, d_gain_two, d_gain_three, d_gain_four], axis=1)
-    kv_width = w_key.shape[1]
-    empty_kv = jnp.zeros((model_dim, kv_width), jnp.float32)
-    key_full = lax.dynamic_update_slice_in_dim(empty_kv, key_fold, kv_first, 1)
-    value_full = lax.dynamic_update_slice_in_dim(empty_kv, value_fold, kv_first, 1)
-    key_sum, value_sum, gain_sum = (
-        lax.psum_scatter(key_full, ("seq", "head", "rows"), scatter_dimension=0, tiled=True),
-        lax.psum_scatter(value_full, ("seq", "head", "rows"), scatter_dimension=0, tiled=True),
-        lax.psum_scatter(gain_terms, ("seq", "head", "rows"), scatter_dimension=0, tiled=True),
+    seq_count = lax.axis_size("seq")
+
+    def own_rows_by_head(terms):
+        width = terms.shape[1]
+        ordered = terms.reshape(seq_count, head_count, row_count, -1, width)
+        ordered = ordered.transpose(0, 2, 1, 3, 4).reshape(model_dim, width)
+        return lax.psum_scatter(ordered, ("seq", "rows"), scatter_dimension=0, tiled=True)
+
+    kv_rows = own_rows_by_head(kv_grad_local)
+    kv_parts = lax.all_to_all(
+        kv_rows.reshape(head_count, -1, 2 * kv_cols), "head", split_axis=0, concat_axis=0, tiled=True
+    )
+    kv_parts = kv_parts.transpose(1, 0, 2)
+    own_count = kv_parts.shape[0]
+    key_sum = kv_parts[:, :, :kv_cols].reshape(own_count, -1)
+    value_sum = kv_parts[:, :, kv_cols:].reshape(own_count, -1)
+    gain_sum = lax.psum_scatter(
+        own_rows_by_head(gain_terms), "head", scatter_dimension=0, tiled=True
     )
     ffcols = w_gate.shape[1]
     gate_first = 2 * qcols

time: 2140 us -> 1000 us (0.47)
  waiting for transfers between devices: 1730 us -> 635 us
  blocking collectives: 121 us -> 79.8 us
    reduce_scatter x2 -> x1, waiting for transfers between devices: 1220 us -> 30.7 us  [own_rows_by_head(): lax.psum_scatter(ordered, ('seq', 'rows'), scatter_dimension=0, tiled=True)]
    unnamed x15 -> x16, waiting for transfers between devices: 51.7 us -> 110 us
    unnamed x1, blocking collectives: 64.9 us -> 24.1 us
    reduce_scatter x1, waiting for transfers between devices: 0.02 us -> 26 us  [per_device(): lax.psum_scatter(jnp.concatenate([d_keys, d_values], axis=1).astype(jnp.b...]
  transfers between devices with their start and end apart: 14 -> 15, of which waited for: 12 -> 14; matrix products, arithmetic and copies ran while one was open for 5% -> 8% of each run, Pallas kernels for 0% -> 0%
where the time goes in v1:
time: 1000 us; the launch traced here: 995 us
  waiting for transfers between devices  635 us (64%)
  matrix products  147 us (15%)
  other arithmetic  82.2 us (8%)
  blocking collectives  79.8 us (8%)
  local copies, waits for them, and re-layouts  27.5 us (3%)
  between operations  15.9 us (2%)
    reduce_scatter x4, waiting for transfers between devices, sum_heads(): lax.psum_scatter(term_fn(jnp.int32(0), tok_block * lax.axis_size('head'))...  295 us
    all_gather x4, waiting for transfers between devices, gather_heads(): return lax.all_gather(values, 'head', axis=0, tiled=True)  157 us
    unnamed x16, waiting for transfers between devices  110 us
    another operation x4, other arithmetic  32.6 us
    reduce_scatter x1, waiting for transfers between devices, own_rows_by_head(): lax.psum_scatter(ordered, ('seq', 'rows'), scatter_dimension=0, tiled=True)  30.7 us
    dot_general x1, matrix products, per_device(): jnp.einsum('upfa,ypa->pfuy', attended_layout, backward_values_layout, pre...  27.4 us
    reduce_scatter x1, waiting for transfers between devices, per_device(): lax.psum_scatter(jnp.concatenate([d_keys, d_values], axis=1).astype(jnp.b...  26 us
    unnamed x1, blocking collectives  24.1 us
  transfers between devices with their start and end apart: 15, of which 14 were waited for; matrix products, arithmetic and copies ran while one was open for 8% of the time, Pallas kernels for 0%

profile of v1, /device:TPU:0, one launch (start us, length us, event | category | flops | bytes accessed | tf_op | source)
XLA Modules:
  0.0 995.1 jit_solution(1179021911307472106)
XLA Ops:
  12.2 5.9 all_gather.42
  18.9 5.8 all_gather.41
  25.1 7.9 all_gather.40
  33.0 7.7 all_gather.45
  43.6 24.4 %all-gather.7.cloned.1.call-done = bf16[1024,1024]{1,0:T(8,128)(2,1)} async-done(((bf16[128,1024]{1,0:T(8,128)(2,1)}), bf16[1024,1024]{1,0:T(8,128)(2,1)}) %all-gather.7.cloned.1.call-update) | async-done | bytes 2097168 | tf_op jit(solution)/shard_map/all_gather | solution.py:90
  68.0 2.9 fusion.105
  73.1 5.5 compare_and_fusion
  83.0 8.6 all-gather.11.cloned.1.call-done
  91.6 15.8 %fusion.5 = (f32[2,1024]{1,0:T(2,128)S(1)}, f32[4096,1024,2]{1,0,2:T(8,128)}) fusion(pred[1024,4096]{0,1:T(8,128)(4,1)} %compare_and_fusion, bf16[1024,2,128]{2,0,1:T(8,128)(2,1)S(1)} %fusion.63, bf16[4096,128]{0,1:T(8,128)(2,1)} %all-gather.11.cloned.1.call-done), kind=kOutput, calls=%fused_computation.11 | convolution fusion | flops 2181036032 | bytes 39329792 | tf_op jit(solution)/shard_map/upfa,ypa->pfuy/dot_general | solution.py:113
  107.4 15.9 %fusion.4 = f32[2,1024]{1,0:T(2,128)S(1)} fusion(f32[4096,1024,2]{1,0,2:T(8,128)} %get-tuple-element.118, f32[2,1024]{1,0:T(2,128)S(1)} %get-tuple-element.117, pred[1024,4096]{0,1:T(8,128)(4,1)S(1)} %copy-done.2), kind=kLoop, calls=%fused_computation.10 | loop fusion | flops 41940992 | bytes 37765120 | tf_op jit(solution)/shard_map/reduce_sum | solution.py:120
  123.3 20.0 %fusion.58 = bf16[128,2,1024]{2,0,1:T(8,128)(2,1)S(1)} fusion(bf16[4096,128]{0,1:T(8,128)(2,1)} %all-gather.9.cloned.1.call-done, f32[2,1024]{1,0:T(2,128)S(1)} %fusion.4, f32[2,1024]{1,0:T(2,128)S(1)} %get-tuple-element.117, f32[4096,1024,2]{1,0,2:T(8,128)} %get-tuple-element.118, pred[1024,4096]{0,1:T(8,128)(4,1)} %compare_and_fusion), kind=kOutput, calls=%fused_computation.92 | convolution fusion | flops 2198077440 | bytes 39337984 | tf_op jit(solution)/shard_map/xlrn,nxt->rxlt/dot_general | solution.py:201
  143.3 2.3 convolution_convert_fusion.2
  145.6 76.2 %reduce-scatter.14.cloned.1.call-done = bf16[128,1024]{1,0:T(8,128)(2,1)} async-done(((bf16[1024,1024]{1,0:T(8,128)(2,1)}), bf16[128,1024]{1,0:T(8,128)(2,1)}) %reduce-scatter.14.cloned.1.call-update) | async-done | bytes 262160 | tf_op jit(solution)/shard_map/reduce_scatter | solution.py:94
  224.2 1.9 multiply_convert_fusion.4
  226.2 7.7 all_gather.47
  233.9 11.5 %all_gather.48 = bf16[1024,384]{1,0:T(8,128)(2,1)S(1)} all-gather(bf16[256,384]{1,0:T(8,128)(2,1)S(1)} %copy-done.32), channel_id=1, replica_groups=mesh['seq'=4,'head'=8,'rows'=4] {'rows'}, dimensions={0}, use_global_device_ids=true | all-gather | bytes 983040 | tf_op jit(solution)/shard_map/all_gather | solution.py:162
  245.4 9.1 all_gather.49
  254.6 27.2 %all-gather.13.cloned.1.call-done = bf16[1024,1024]{1,0:T(8,128)(2,1)} async-done(((bf16[128,1024]{1,0:T(8,128)(2,1)}), bf16[1024,1024]{1,0:T(8,128)(2,1)}) %all-gather.13.cloned.1.call-update) | async-done | bytes 2097168 | tf_op jit(solution)/shard_map/all_gather | solution.py:90
  281.8 4.5 fusion.184
  286.3 4.1 multiply_convert_fusion.1
  291.3 3.7 convolution_convert_fusion
  295.1 73.0 %reduce-scatter.16.cloned.1.call-done = bf16[128,1024]{1,0:T(8,128)(2,1)} async-done(((bf16[1024,1024]{1,0:T(8,128)(2,1)}), bf16[128,1024]{1,0:T(8,128)(2,1)}) %reduce-scatter.16.cloned.1.call-update) | async-done | bytes 262160 | tf_op jit(solution)/shard_map/reduce_scatter | solution.py:94
  373.0 52.8 %all-gather.15.cloned.1.call-done = bf16[1024,1024]{1,0:T(8,128)(2,1)} async-done(((bf16[128,1024]{1,0:T(8,128)(2,1)}), bf16[1024,1024]{1,0:T(8,128)(2,1)}) %all-gather.15.cloned.1.call-update) | async-done | bytes 2097168 | tf_op jit(solution)/shard_map/all_gather | solution.py:90
  425.8 6.2 multiply_convert_fusion
  432.0 2.3 fusion.182
  434.4 3.8 add_convert_fusion
  438.3 73.0 %reduce-scatter.18.cloned.1.call-done = bf16[128,1024]{1,0:T(8,128)(2,1)} async-done(((bf16[1024,1024]{1,0:T(8,128)(2,1)}), bf16[128,1024]{1,0:T(8,128)(2,1)}) %reduce-scatter.18.cloned.1.call-update) | async-done | bytes 262160 | tf_op jit(solution)/shard_map/reduce_scatter | solution.py:94
  513.2 2.8 fusion.86
  517.8 53.0 %all-gather.17.cloned.1.call-done = bf16[1024,1024]{1,0:T(8,128)(2,1)} async-done(((bf16[128,1024]{1,0:T(8,128)(2,1)}), bf16[1024,1024]{1,0:T(8,128)(2,1)}) %all-gather.17.cloned.1.call-update) | async-done | bytes 2097168 | tf_op jit(solution)/shard_map/all_gather | solution.py:90
  570.8 2.7 convolution_convert_fusion.8
  573.6 17.8 %fusion.19 = bf16[4096,128]{0,1:T(8,128)(2,1)S(1)} fusion(bf16[1024,2,128]{0,2,1:T(8,128)(2,1)S(1)} %bitcast.194, f32[2,1024]{1,0:T(2,128)S(1)} %fusion.4, f32[2,1024]{1,0:T(2,128)S(1)} %get-tuple-element.117, f32[4096,1024,2]{1,0,2:T(8,128)} %get-tuple-element.118, pred[1024,4096]{0,1:T(8,128)(4,1)S(1)} %copy-done.3), kind=kOutput, calls=%fused_computation.23 | convolution fusion | flops 2198339584 | bytes 39337984 | tf_op jit(solution)/shard_map/rnej,ernu->jru/dot_general | solution.py:279
  591.4 27.4 %fusion.1 = (f32[2,1024]{1,0:T(2,128)S(1)}, f32[4096,1024,2]{1,0,2:T(8,128)}) fusion(f32[2,1024]{1,0:T(2,128)S(1)} %fusion.4, f32[2,1024]{1,0:T(2,128)S(1)} %get-tuple-element.117, f32[4096,1024,2]{1,0,2:T(8,128)} %get-tuple-element.118, pred[1024,4096]{0,1:T(8,128)(4,1)S(1)} %copy-done.3, bf16[1024,2,128]{0,2,1:T(8,128)(2,1)S(1)} %bitcast.195, ...), kind=kOutput, calls=%fused_computation.5 | convolution fusion | flops 2206201856 | bytes 72900608 | tf_op jit(solution)/shard_map/upfa,ypa->pfuy/dot_general | solution.py:259
  618.8 30.0 %fusion.6 = bf16[2,1024,4096]{1,2,0:T(8,128)(2,1)} fusion(f32[4096,1024,2]{1,0,2:T(8,128)} %get-tuple-element.118, f32[4096,1024,2]{1,0,2:T(8,128)} %get-tuple-element.122, f32[2,1024]{1,0:T(2,128)S(1)} %get-tuple-element.121, f32[2,1024]{1,0:T(2,128)S(1)} %fusion.4, f32[2,1024]{1,0:T(2,128)S(1)} %get-tuple-element.117, pred[1024,4096]{0,1:T(8,128)(4,1)} %compare_and_fusion), kind=kLoop, calls=%fused_computation.12 | loop fusion | flops 92274688 | bytes 88104960 | tf_op jit(solution)/shard_map/reshape.20
  648.7 11.5 %fusion.22 = bf16[4096,128]{0,1:T(8,128)(2,1)S(1)} fusion(bf16[1024,2,128]{2,0,1:T(8,128)(2,1)S(1)} %copy-done.16, bf16[2,1024,4096]{1,2,0:T(8,128)(2,1)} %fusion.6), kind=kOutput, calls=%fused_computation.24 | convolution fusion | flops 2148007936 | bytes 18350080 | tf_op jit(solution)/shard_map/rnej,ernu->jru/dot_general | solution.py:276
  661.8 26.0 %reduce-scatter.20.cloned.1.call-done = bf16[1024,256]{0,1:T(8,128)(2,1)} async-done(((bf16[4096,256]{0,1:T(8,128)(2,1)}), bf16[1024,256]{0,1:T(8,128)(2,1)}) %reduce-scatter.20.cloned.1.call-update) | async-done | bytes 524304 | tf_op jit(solution)/shard_map/reduce_scatter | solution.py:282
  692.8 10.2 %fusion.57 = f32[1024,2,128]{2,0,1:T(8,128)S(1)} fusion(bf16[2,1024,4096]{1,2,0:T(8,128)(2,1)} %fusion.6, bf16[4096,128]{0,1:T(8,128)(2,1)S(1)} %copy-done.19), kind=kOutput, calls=%fused_computation.91 | convolution fusion | flops 2147745792 | bytes 18874368 | tf_op jit(solution)/shard_map/xlrn,nxt->rxlt/dot_general | solution.py:269
  708.8 1.9 fusion.56
  710.8 1.9 fusion.55
  712.7 1.9 fusion.54
  714.6 5.6 copy.131
  721.5 2.6 convolution_convert_fusion.1
  724.2 30.7 %reduce-scatter.24.cloned.1.call-done = f32[64,256]{1,0:T(8,128)} async-done(((f32[1024,256]{1,0:T(8,128)}), f32[64,256]{1,0:T(8,128)}) %reduce-scatter.24.cloned.1.call-update) | async-done | bytes 65552 | tf_op jit(solution)/shard_map/reduce_scatter | solution.py:325
  754.9 6.7 all-to-all-start
  763.3 6.2 all-to-all-done
  770.1 51.7 %reduce-scatter.26.cloned.1.call-done = bf16[64,1664]{1,0:T(8,128)(2,1)} async-done(((bf16[1024,1664]{1,0:T(8,128)(2,1)}), bf16[64,1664]{1,0:T(8,128)(2,1)}) %reduce-scatter.26.cloned.1.call-update) | async-done | bytes 213008
  826.8 73.2 %reduce-scatter.22.cloned.1.call-done = bf16[128,1024]{1,0:T(8,128)(2,1)} async-done(((bf16[1024,1024]{1,0:T(8,128)(2,1)}), bf16[128,1024]{1,0:T(8,128)(2,1)}) %reduce-scatter.22.cloned.1.call-update) | async-done | bytes 262160 | tf_op jit(solution)/shard_map/reduce_scatter | solution.py:94
  904.1 58.4 %reduce-scatter.28.cloned.1.call-done = f32[64,4]{1,0:T(8,128)} async-done(((f32[1024,4]{1,0:T(8,128)}), f32[64,4]{1,0:T(8,128)}) %reduce-scatter.28.cloned.1.call-update) | async-done | bytes 1040
  963.4 24.1 %all-reduce = f32[64,4]{0,1:T(4,128)S(1)} all-reduce(f32[64,4]{0,1:T(4,128)S(1)} %copy.134), channel_id=10, replica_groups=mesh['seq'=4,'head'=8,'rows'=4] {'head'}, use_global_device_ids=true, to_apply=%region_27.28.clone | all-reduce | flops 256 | bytes 2048
  (239 shorter events, 53.1 us)
Async XLA Ops:
  7.2 25.7 %copy-start.35 = (bf16[256,256]{1,0:T(8,128)(2,1)S(1)}, bf16[256,256]{1,0:T(8,128)(2,1)}, u32[]{:S(2)}) copy-start(bf16[256,256]{1,0:T(8,128)(2,1)} %param.19) | copy-start | bytes 393220
  7.2 60.8 %all-gather.7.cloned.1.call-start = ((), (), s32[]{:S(2)}) async-start(), calls=%async_computation.9 | async-start | bytes 2359296 | tf_op jit(solution)/shard_map/all_gather | solution.py:90
  11.3 80.3 %all-gather.11.cloned.1.call-start = ((), (), s32[]{:S(2)}) async-start(), calls=%async_computation.11 | async-start | bytes 1310720 | tf_op jit(solution)/shard_map/all_gather | solution.py:104
  24.8 46.2 %copy-start.47 = (f32[64]{0:T(128)}, f32[64]{0:T(128)S(1)}, u32[]{:S(2)}) copy-start(f32[64]{0:T(128)S(1)} %multiply_exponential_fusion) | copy-start | bytes 772
  40.7 30.3 %copy-start.37 = (f32[1024]{0:T(1024)}, f32[1024]{0:T(1024)S(1)}, u32[]{:S(2)}) copy-start(f32[1024]{0:T(1024)S(1)} %subtract_convert_fusion.1) | copy-start | bytes 12292
  41.0 30.0 %copy-start.25 = (bf16[1024,128]{1,0:T(8,128)(2,1)}, bf16[1024,128]{1,0:T(8,128)(2,1)S(1)}, u32[]{:S(2)}) copy-start(bf16[1024,128]{1,0:T(8,128)(2,1)S(1)} %multiply_convert_fusion.5) | copy-start | bytes 786436
  41.2 29.7 %copy-start.27 = (bf16[1024,128]{1,0:T(8,128)(2,1)}, bf16[1024,128]{1,0:T(8,128)(2,1)S(1)}, u32[]{:S(2)}) copy-start(bf16[1024,128]{1,0:T(8,128)(2,1)S(1)} %multiply_convert_fusion.6) | copy-start | bytes 786436
  41.7 29.3 %copy-start.23 = (bf16[1024,256]{1,0:T(8,128)(2,1)}, bf16[1024,256]{1,0:T(8,128)(2,1)S(1)}, u32[]{:S(2)}) copy-start(bf16[1024,256]{1,0:T(8,128)(2,1)S(1)} %multiply_convert_fusion.3) | copy-start | bytes 1572868
  43.6 38.5 %copy-start.9 = (f32[1024,64]{1,0:T(8,128)}, f32[1024,64]{1,0:T(8,128)S(1)}, u32[]{:S(2)}) copy-start(f32[1024,64]{1,0:T(8,128)S(1)} %get-tuple-element.111) | copy-start | bytes 786436
  43.6 38.5 %copy-start.11 = (f32[1024,64]{1,0:T(8,128)}, f32[1024,64]{1,0:T(8,128)S(1)}, u32[]{:S(2)}) copy-start(f32[1024,64]{1,0:T(8,128)S(1)} %get-tuple-element.112) | copy-start | bytes 786436
  73.0 50.2 %all-gather.9.cloned.1.call-start = ((), (), s32[]{:S(2)}) async-start(), calls=%async_computation.10 | async-start | bytes 1310720 | tf_op jit(solution)/shard_map/all_gather | solution.py:105
  82.7 24.7 %copy-start.15 = (bf16[1024,2,128]{2,0,1:T(8,128)(2,1)}, bf16[1024,2,128]{2,0,1:T(8,128)(2,1)S(1)}, u32[]{:S(2)}) copy-start(bf16[1024,2,128]{2,0,1:T(8,128)(2,1)S(1)} %fusion.63) | copy-start | bytes 1572868
  82.7 139.2 %reduce-scatter.14.cloned.1.call-start = ((), (), s32[]{:S(2)}) async-start(), calls=%async_computation.12 | async-start | bytes 2359296 | tf_op jit(solution)/shard_map/reduce_scatter | solution.py:94
  145.5 77.4 %copy-start.4 = (bf16[128,1024]{1,0:T(8,128)(2,1)S(1)}, bf16[128,1024]{1,0:T(8,128)(2,1)}, u32[]{:S(2)}) copy-start(bf16[128,1024]{1,0:T(8,128)(2,1)} %param.14) | copy-start | bytes 786436
  145.5 77.5 %copy-start.36 = (f32[1024]{0:T(1024)S(1)}, f32[1024]{0:T(1024)}, u32[]{:S(2)}) copy-start(f32[1024]{0:T(1024)} %param.24) | copy-start | bytes 12292
  145.5 78.7 %copy-start.39 = (f32[1024]{0:T(1024)S(1)}, f32[1024]{0:T(1024)}, u32[]{:S(2)}) copy-start(f32[1024]{0:T(1024)} %param.25) | copy-start | bytes 12292
  145.5 80.7 %copy-start.31 = (bf16[256,384]{1,0:T(8,128)(2,1)S(1)}, bf16[256,384]{1,0:T(8,128)(2,1)}, u32[]{:S(2)}) copy-start(bf16[256,384]{1,0:T(8,128)(2,1)} %param.20) | copy-start | bytes 589828
  145.6 88.3 %copy-start.32 = (bf16[256,384]{1,0:T(8,128)(2,1)S(1)}, bf16[256,384]{1,0:T(8,128)(2,1)}, u32[]{:S(2)}) copy-start(bf16[256,384]{1,0:T(8,128)(2,1)} %param.21) | copy-start | bytes 589828
  145.6 136.2 %all-gather.13.cloned.1.call-start = ((), (), s32[]{:S(2)}) async-start(), calls=%async_computation.13 | async-start | bytes 2359296 | tf_op jit(solution)/shard_map/all_gather | solution.py:90
  226.2 141.8 %reduce-scatter.16.cloned.1.call-start = ((), (), s32[]{:S(2)}) async-start(), calls=%async_computation.14 | async-start | bytes 2359296 | tf_op jit(solution)/shard_map/reduce_scatter | solution.py:94
  295.0 74.1 %copy-start.14 = (bf16[128,1024]{1,0:T(8,128)(2,1)S(1)}, bf16[128,1024]{1,0:T(8,128)(2,1)}, u32[]{:S(2)}) copy-start(bf16[128,1024]{1,0:T(8,128)(2,1)} %param.27) | copy-start | bytes 786436
  295.0 74.1 %copy-start.40 = (f32[1024]{0:T(1024)S(1)}, f32[1024]{0:T(1024)}, u32[]{:S(2)}) copy-start(f32[1024]{0:T(1024)} %param.26) | copy-start | bytes 12292
  295.0 130.8 %all-gather.15.cloned.1.call-start = ((), (), s32[]{:S(2)}) async-start(), calls=%async_computation.15 | async-start | bytes 2359296 | tf_op jit(solution)/shard_map/all_gather | solution.py:90
  372.8 138.5 %reduce-scatter.18.cloned.1.call-start = ((), (), s32[]{:S(2)}) async-start(), calls=%async_computation.16 | async-start | bytes 2359296 | tf_op jit(solution)/shard_map/reduce_scatter | solution.py:94
  438.2 73.0 %copy-start.6 = (bf16[128,1024]{1,0:T(8,128)(2,1)S(1)}, bf16[128,1024]{1,0:T(8,128)(2,1)}, u32[]{:S(2)}) copy-start(bf16[128,1024]{1,0:T(8,128)(2,1)} %reduce-scatter.14.cloned.1.call-done) | copy-start | bytes 786436
  438.2 75.0 %copy-start.13 = (bf16[128,1024]{1,0:T(8,128)(2,1)S(1)}, bf16[128,1024]{1,0:T(8,128)(2,1)}, u32[]{:S(2)}) copy-start(bf16[128,1024]{1,0:T(8,128)(2,1)} %reduce-scatter.16.cloned.1.call-done) | copy-start | bytes 786436
  438.3 132.5 %all-gather.17.cloned.1.call-start = ((), (), s32[]{:S(2)}) async-start(), calls=%async_computation.17 | async-start | bytes 2359296 | tf_op jit(solution)/shard_map/all_gather | solution.py:90
  513.2 57.6 %copy-start.22 = (bf16[1024,256]{1,0:T(8,128)(2,1)S(1)}, bf16[1024,256]{1,0:T(8,128)(2,1)}, u32[]{:S(2)}) copy-start(bf16[1024,256]{1,0:T(8,128)(2,1)} %all_gather.45) | copy-start | bytes 1572868
  517.8 170.1 %reduce-scatter.20.cloned.1.call-start = ((), (), s32[]{:S(2)}) async-start(), calls=%async_computation.18 | async-start | bytes 2621440 | tf_op jit(solution)/shard_map/reduce_scatter | solution.py:282
  618.8 30.0 %copy-start.16 = (bf16[1024,2,128]{2,0,1:T(8,128)(2,1)S(1)}, bf16[1024,2,128]{2,0,1:T(8,128)(2,1)}, u32[]{:S(2)}) copy-start(bf16[1024,2,128]{2,0,1:T(8,128)(2,1)} %copy-done.15) | copy-start | bytes 1572868
  661.7 27.2 %copy-start.38 = (f32[1024]{0:T(1024)S(1)}, f32[1024]{0:T(1024)}, u32[]{:S(2)}) copy-start(f32[1024]{0:T(1024)} %copy-done.37) | copy-start | bytes 12292
  661.7 27.2 %copy-start.48 = (f32[64]{0:T(128)S(1)}, f32[64]{0:T(128)}, u32[]{:S(2)}) copy-start(f32[64]{0:T(128)} %copy-done.47) | copy-start | bytes 772
  661.7 28.7 %copy-start.52 = (bf16[1024,1024]{1,0:T(8,128)(2,1)S(1)}, bf16[1024,1024]{1,0:T(8,128)(2,1)}, u32[]{:S(2)}) copy-start(bf16[1024,1024]{1,0:T(8,128)(2,1)} %all-gather.7.cloned.1.call-done) | copy-start | bytes 6291460
  661.8 93.1 %reduce-scatter.24.cloned.1.call-start = ((), (), s32[]{:S(2)}) async-start(), calls=%async_computation.20 | async-start | bytes 1114112 | tf_op jit(solution)/shard_map/reduce_scatter | solution.py:325
  692.4 129.4 %reduce-scatter.26.cloned.1.call-start = ((), (), s32[]{:S(2)}) async-start(), calls=%async_computation.21 | async-start | bytes 3620864
  720.3 179.8 %reduce-scatter.22.cloned.1.call-start = ((), (), s32[]{:S(2)}) async-start(), calls=%async_computation.19 | async-start | bytes 2359296 | tf_op jit(solution)/shard_map/reduce_scatter | solution.py:94
  724.1 37.6 %copy-start.61 = (u32[128]{0:T(128)S(1)}, u32[128]{0:T(128)}, u32[]{:S(2)}) copy-start(u32[128]{0:T(128)} %constant.210) | copy-start | bytes 1540
  724.1 38.8 %copy-start.42 = (f32[1024]{0:T(1024)S(1)}, f32[1024]{0:T(1024)}, u32[]{:S(2)}) copy-start(f32[1024]{0:T(1024)} %get-tuple-element.84) | copy-start | bytes 12292
  724.1 38.9 %copy-start.44 = (f32[1024]{0:T(1024)S(1)}, f32[1024]{0:T(1024)}, u32[]{:S(2)}) copy-start(f32[1024]{0:T(1024)} %get-tuple-element.80) | copy-start | bytes 12292
  724.1 39.1 %copy-start.43 = (f32[1024]{0:T(1024)S(1)}, f32[1024]{0:T(1024)}, u32[]{:S(2)}) copy-start(f32[1024]{0:T(1024)} %get-tuple-element.78) | copy-start | bytes 12292
  754.9 14.6 %all-to-all-start = ((f32[8,8,256]{2,1,0:T(8,128)}), f32[8,8,256]{2,1,0:T(8,128)S(1)}, u32[]{:S(2)}, u32[]{:S(2)}) async-start(f32[8,8,256]{2,1,0:T(8,128)} %bitcast.187), calls=%async_computation.6 | async-start | bytes 131072 | tf_op jit(solution)/shard_map/all_to_all | solution.py:328
  761.6 201.0 %reduce-scatter.28.cloned.1.call-start = ((), (), s32[]{:S(2)}) async-start(), calls=%async_computation.22 | async-start | bytes 557056
  823.0 77.0 %copy-start.5 = (bf16[128,1024]{1,0:T(8,128)(2,1)S(1)}, bf16[128,1024]{1,0:T(8,128)(2,1)}, u32[]{:S(2)}) copy-start(bf16[128,1024]{1,0:T(8,128)(2,1)} %param.14) | copy-start | bytes 786436
  823.0 77.0 %copy-start.41 = (f32[1024]{0:T(1024)S(1)}, f32[1024]{0:T(1024)}, u32[]{:S(2)}) copy-start(f32[1024]{0:T(1024)} %param.23) | copy-start | bytes 12292
  823.1 77.0 %copy-start.46 = (f32[128]{0:T(128)S(1)}, f32[128]{0:T(128)}, u32[]{:S(2)}) copy-start(f32[128]{0:T(128)} %copy-done.45) | copy-start | bytes 1540
  825.4 77.8 %copy-start.50 = (f32[128]{0:T(128)S(1)}, f32[128]{0:T(128)}, u32[]{:S(2)}) copy-start(f32[128]{0:T(128)} %copy-done.49) | copy-start | bytes 1540
  825.4 77.8 %copy-start.8 = (f32[128,1024]{1,0:T(8,128)S(1)}, f32[128,1024]{1,0:T(8,128)}, u32[]{:S(2)}) copy-start(f32[128,1024]{1,0:T(8,128)} %copy-done.7) | copy-start | bytes 1572868
  901.3 86.8 %copy-start.1 = (bf16[256,1024]{1,0:T(8,128)(2,1)S(1)}, bf16[256,1024]{1,0:T(8,128)(2,1)}, u32[]{:S(2)}) copy-start(bf16[256,1024]{1,0:T(8,128)(2,1)} %param.18) | copy-start | bytes 1572868
  (36 other events, 189.2 us)
Sparse Core Ops, SparseCore 0:
  11.4 56.6 all-gather.6
  73.2 18.3 all-gather.10
  93.8 21.6 all-gather.8
  145.7 76.1 reduce-scatter.13
  226.3 55.4 all-gather.12
  295.1 72.8 reduce-scatter.15
  372.9 52.8 all-gather.14
  438.4 72.8 reduce-scatter.17
  517.9 52.8 all-gather.16
  661.9 25.9 reduce-scatter.19
  692.5 62.3 reduce-scatter.23
  757.2 64.6 reduce-scatter.25
  826.0 74.0 reduce-scatter.21
  903.3 59.2 reduce-scatter.27

commit v2 on v0

v2 whole, which is shorter than its diff:
```python
import math

import jax
import jax.numpy as jnp
from jax import lax
from jax.experimental import pallas as pl
from jax.experimental.pallas import tpu as pltpu
from jax.sharding import Mesh
from jax.sharding import PartitionSpec as P

DH = 128
QEXP_MODEL = 10
QEXP_HIDDEN = 11
CAP = 50.0
EPSILON = 1e-06
THETA = 10000.0
SCALE = DH ** (-0.5)
AXES = ("x", "yh", "z", "yl", "c")
BY_ID = pl.DeviceIdType.MESH
F32 = jnp.float32
BF16 = jnp.bfloat16
VM = pl.BlockSpec(memory_space=pltpu.VMEM)
SM = pl.BlockSpec(memory_space=pltpu.SMEM)
VMEM_LIMIT = 56 * 2**20


def here():
    return tuple(lax.axis_index(name) for name in AXES)


def z_device(step):
    x, yh, z, yl, c = here()
    return (x, yh, lax.rem(z + step, 4), yl, c)


def y_device(step):
    x, yh, z, yl, c = here()
    y = lax.rem(yh * 2 + yl + step, 4)
    return (x, lax.div(y, 2), z, lax.rem(y, 2), c)


def x_device(step):
    x, yh, z, yl, c = here()
    return (lax.rem(x + step, 4), yh, z, yl, c)


def sibling():
    x, yh, z, yl, c = here()
    return (x, yh, z, yl, 1 - c)


def greet(devices):
    barrier = pltpu.get_barrier_semaphore()
    for device in devices:
        pl.semaphore_signal(barrier, inc=1, device_id=device, device_id_type=BY_ID)
    pl.semaphore_wait(barrier, len(devices))


class Links:
    def __init__(self, send_sems, recv_sems):
        self.send_sems = send_sems
        self.recv_sems = recv_sems
        self.used = 0

    def plan(self, source, target, device):
        at = self.used
        self.used += 1
        return pltpu.make_async_remote_copy(
            src_ref=source,
            dst_ref=target,
            send_sem=self.send_sems.at[at],
            recv_sem=self.recv_sems.at[at],
            device_id=device,
            device_id_type=BY_ID,
        )

    def send(self, source, target, device):
        copy = self.plan(source, target, device)
        copy.start()
        return copy


def dot(left, right):
    return lax.dot_general(left, right, (((1,), (0,)), ((), ())), preferred_element_type=F32)


def dot_nt(left, right):
    return lax.dot_general(left, right, (((1,), (1,)), ((), ())), preferred_element_type=F32)


def dot_tn(left, right):
    return lax.dot_general(left, right, (((0,), (0,)), ((), ())), preferred_element_type=F32)


def quantized(weight, exponent, bits):
    shift = 8 - bits
    code = jnp.clip(jnp.floor(weight.astype(F32) * 2.0**exponent) + 128.0, 0.0, 255.0)
    if shift:
        code = (
            jnp.minimum(jnp.floor((code + 2.0 ** (shift - 1)) * 2.0 ** (-shift)), 2.0**bits - 1.0)
            * 2.0**shift
        )
    return ((code - 128.0) * 2.0 ** (-exponent)).astype(BF16)


def inverse_rms(values):
    return lax.rsqrt(jnp.mean(values * values, axis=-1, keepdims=True) + EPSILON)


def rms_back(values, gain, incoming):
    inverse = inverse_rms(values)
    scaled = incoming * gain
    inner = jnp.mean(scaled * values, axis=-1, keepdims=True)
    into = inverse * (scaled - values * (inverse * inverse) * inner)
    gain_part = jnp.sum(incoming * values * inverse, axis=0, keepdims=True)
    return into, gain_part


def swap_halves(values):
    half = values.shape[-1] // 2
    return jnp.concatenate([values[..., half:], values[..., :half]], axis=-1)


class Gather:
    def __init__(self, links, buffer, lead=()):
        x, yh, z, yl, c = here()
        self.links = links
        self.buffer = buffer
        self.lead = lead
        own = buffer.at[lead + (yh, yl * 2 + c)]
        self.ring = {step: links.send(own, own, y_device(step)) for step in (2, 1, 3)}
        self.pair = links.send(own, own, sibling())
        self.passed = []

    def forward(self):
        x, yh, z, yl, c = here()
        for step in (1, 3, 2):
            self.ring[step].wait_recv()
            origin = lax.rem(yh * 2 + yl + 4 - step, 4)
            block = self.buffer.at[
                self.lead + (lax.div(origin, 2), lax.rem(origin, 2) * 2 + c)
            ]
            self.passed.append(self.links.send(block, block, sibling()))

    def finish(self):
        self.pair.wait()
        for step in (1, 3, 2):
            self.ring[step].wait_send()
        for copy in self.passed:
            copy.wait()


def call(body, name, cid, outs, specs, scratch, sems, flops=0, nbytes=0):
    shapes = tuple(jax.ShapeDtypeStruct(shape, kind) for shape, kind in outs)
    return pl.pallas_call(
        body,
        name=name,
        out_shape=shapes,
        in_specs=specs,
        out_specs=tuple(VM for _ in outs),
        scratch_shapes=list(scratch)
        + [pltpu.SemaphoreType.DMA((sems,)), pltpu.SemaphoreType.DMA((sems,))],
        compiler_params=pltpu.CompilerParams(
            collective_id=cid, has_side_effects=True, vmem_limit_bytes=VMEM_LIMIT
        ),
    )


def qkv_kernel(
    tokens, gain, w_query, w_key, w_value, lengths,
    xn_all, wq_all, wkv_all, q_out, kv_out, cos_out, sin_out,
    send_sems, recv_sems,
):
    x, yh, z, yl, c = here()
    links = Links(send_sems, recv_sems)
    xin = tokens[...].astype(F32)
    xn_all[z] = (xin * inverse_rms(xin) * gain[...]).astype(BF16)
    for group in range(2):
        first = pl.multiple_of(group * 512 + z * 128, 128)
        wkv_all[yl * 2 + c, :, pl.ds(group * 128, 128)] = quantized(
            w_key[:, pl.ds(first, 128)], QEXP_MODEL, 8
        )
        wkv_all[yl * 2 + c, :, pl.ds(256 + group * 128, 128)] = quantized(
            w_value[:, pl.ds(first, 128)], QEXP_MODEL, 8
        )
    wq_all[yh, yl * 2 + c] = quantized(w_query[...], QEXP_MODEL, 8)
    greet([z_device(s) for s in (1, 2, 3)] + [y_device(s) for s in (1, 2, 3)] + [sibling()])
    ring = {s: links.send(xn_all.at[z], xn_all.at[z], z_device(s)) for s in (2, 1, 3)}
    own = wkv_all.at[yl * 2 + c]
    near = links.send(own, own, (x, yh, z, 1 - yl, c))
    pair = links.send(own, own, sibling())
    gather = Gather(links, wq_all)
    start = lengths[0, 0]
    half_lane = lax.rem(lax.broadcasted_iota(jnp.int32, (128, 128), 1), 64).astype(F32)
    freqs = jnp.exp(half_lane * (-2.0 * math.log(THETA) / DH))
    row = lax.broadcasted_iota(jnp.int32, (128, 128), 0)
    lane = lax.broadcasted_iota(jnp.int32, (128, 128), 1)
    for block in range(4):
        tok = row + (yh * 2048 + block * 512 + yl * 256 + c * 128)
        pos = jnp.where(tok >= start, tok - start, tok)
        angle = pos.astype(F32) * freqs
        cos_out[block] = jnp.cos(angle)
        sine = jnp.sin(angle)
        sin_out[block] = jnp.where(lane < 64, -sine, sine)
    near.wait_recv()
    other = wkv_all.at[(1 - yl) * 2 + c]
    passed = links.send(other, other, sibling())
    gather.forward()
    for s in (1, 3, 2):
        ring[s].wait_recv()
    pair.wait_recv()
    passed.wait_recv()
    xa = xn_all[...].reshape(512, 1024)
    cosd = cos_out[...].reshape(512, 128)
    sind = sin_out[...].reshape(512, 128)
    kv_lin = dot(xa, wkv_all[...].reshape(1024, 512))
    for group in range(2):
        key = kv_lin[:, group * 128 : group * 128 + 128]
        key = (key * cosd + swap_halves(key) * sind).astype(BF16)
        kv_out[group, :, :, 0:128] = key.reshape(4, 128, 128)
        value = kv_lin[:, 256 + group * 128 : 256 + group * 128 + 128].astype(BF16)
        kv_out[group, :, :, 128:256] = value.reshape(4, 128, 128)
    gather.finish()
    for group in range(2):
        q_lin = dot(xa, wq_all[group].reshape(1024, 256))
        for head in range(2):
            query = q_lin[:, head * 128 : head * 128 + 128]
            query = ((query * cosd + swap_halves(query) * sind) * SCALE).astype(BF16)
            q_out[group, :, head] = query.reshape(4, 128, 128)
    for copy in ring.values():
        copy.wait_send()
    near.wait_send()
    pair.wait_send()
    passed.wait_send()


def run_qkv(tokens, gain, w_query, w_key, w_value, lengths):
    return call(
        qkv_kernel, "qkv", 1,
        [
            ((4, 128, 1024), BF16), ((2, 4, 256, 256), BF16), ((4, 256, 512), BF16),
            ((2, 4, 2, 128, 128), BF16), ((2, 4, 128, 256), BF16),
            ((4, 128, 128), F32), ((4, 128, 128), F32),
        ],
        [VM] * 5 + [SM], [], 16,
    )(tokens, gain, w_query, w_key, w_value, lengths)


def score_block(query, key, key_base, query_base, start, causal):
    rows, keys = query.shape[0], key.shape[0]
    curved = jnp.tanh(dot_nt(query, key) * (1.0 / CAP))
    weight = jnp.exp(curved * CAP)
    token_q = query_base + lax.rem(lax.broadcasted_iota(jnp.int32, (rows, 1), 0), 128)
    first = jnp.where(token_q >= start, start, 0)
    token_k = key_base
    seen = token_k >= first
    if causal:
        seen = seen & (token_k <= token_q)
    return jnp.where(seen, weight, 0.0).astype(BF16)


def attention_kernel(
    q, kv, w_output, lengths,
    kv_all, attn, recip, wo_all,
    acc, send_sems, recv_sems,
):
    x, yh, z, yl, c = here()
    links = Links(send_sems, recv_sems)
    wo_all[yh, yl * 2 + c] = quantized(w_output[...], QEXP_MODEL, 8)
    greet([y_device(s) for s in (1, 2, 3)] + [sibling()])
    mine = kv_all.at[:, yh, yl, :, c]
    pair = links.send(kv, mine, sibling())
    near = links.send(kv, mine, (x, yh, z, 1 - yl, c))
    far = [
        links.plan(kv, mine, (x, 1, z, 1 - yl, c)),
        links.plan(kv, mine, (x, 1, z, yl, c)),
    ]

    @pl.when(yh == 0)
    def _():
        for copy in far:
            copy.start()

    gather = Gather(links, wo_all)
    kv_all[:, yh, yl, :, c] = kv[...]
    start = lengths[0, 0]
    lane = lax.broadcasted_iota(jnp.int32, (1, 256), 1)
    ones = jnp.ones((256, 128), BF16)

    def add_block(group, block, from_h, from_l, units, first):
        query = q[group, block].reshape(256, 128)
        q_base = yh * 2048 + block * 512 + yl * 256 + c * 128
        total = None
        for unit, causal in units:
            both = kv_all[group, from_h, from_l, unit].reshape(256, 256)
            k_base = from_h * 2048 + unit * 512 + from_l * 256 + lane
            weight = score_block(query, both[:, :128], k_base, q_base, start, causal)
            term = dot(weight, jnp.concatenate([both[:, 128:], ones], axis=1))
            total = term if total is None else total + term
        if first:
            acc[group, block] = total
        else:
            acc[group, block] += total

    def same_half(from_l, first):
        @pl.loop(0, 2)
        def _(group):
            for block in range(4):
                add_block(
                    group, block, yh, from_l,
                    [(unit, False) for unit in range(block)] + [(block, True)], first,
                )

    def other_half(from_l):
        @pl.loop(0, 8)
        def _(at):
            add_block(
                lax.div(at, 4), lax.rem(at, 4), 0, from_l,
                [(unit, False) for unit in range(4)], False,
            )

    pair.wait_recv()
    same_half(yl, True)
    near.wait_recv()
    block = kv_all.at[:, yh, 1 - yl, :, c]
    passed = links.send(block, block, sibling())
    passed.wait_recv()
    same_half(1 - yl, False)
    gather.forward()
    onward = []
    for copy, from_l in zip(far, (1 - yl, yl)):
        block = kv_all.at[:, 0, from_l, :, c]
        onward.append(links.plan(block, block, sibling()))

    @pl.when(yh == 1)
    def _():
        for copy, step, from_l in zip(far, onward, (1 - yl, yl)):
            copy.wait_recv()
            step.start()
            step.wait_recv()
            other_half(from_l)
        for step in onward:
            step.wait_send()

    for group in range(2):
        for block in range(4):
            total = acc[group, block]
            inverse = 1.0 / total[:, 128:256]
            recip[group, block] = inverse
            out = (total[:, :128] * inverse).astype(BF16)
            for head in range(2):
                first = group * 256 + head * 128
                attn[block, :, first : first + 128] = out[head * 128 : head * 128 + 128]
    gather.finish()
    pair.wait_send()
    near.wait_send()
    passed.wait_send()

    @pl.when(yh == 0)
    def _():
        for copy in far:
            copy.wait_send()


def run_attention(q, kv, w_output, lengths):
    return call(
        attention_kernel, "attention", 2,
        [
            ((2, 2, 2, 4, 2, 128, 256), BF16), ((4, 128, 512), BF16),
            ((2, 4, 256, 128), F32), ((2, 4, 256, 256), BF16),
        ],
        [VM] * 3 + [SM], [pltpu.VMEM((2, 4, 256, 256), F32)], 16,
    )(q, kv, w_output, lengths)


def scatter_z(links, partial_of, send_buf, recv_buf):
    x, yh, z, yl, c = here()
    copies = []
    for step in (2, 1, 3):
        send_buf[step - 1] = partial_of(lax.rem(z + step, 4)).astype(BF16)
        copies.append(links.send(send_buf.at[step - 1], recv_buf.at[step - 1], z_device(step)))
    return copies, partial_of(z)


def gather_z(links, buffer):
    x, yh, z, yl, c = here()
    return [links.send(buffer.at[z], buffer.at[z], z_device(s)) for s in (2, 1, 3)]


def outproj_kernel(
    attn, wo_all, tokens, gain_out, gain_in, w_gate, w_up, w_down,
    branch_out, h1_out, hn_all, wf_all,
    send_buf, recv_buf, send_sems, recv_sems,
):
    x, yh, z, yl, c = here()
    links = Links(send_sems, recv_sems)
    greet([z_device(s) for s in (1, 2, 3)] + [y_device(s) for s in (1, 2, 3)] + [sibling()])

    def partial_of(block):
        left = attn[block]
        return dot_nt(left[:, :256], wo_all[0].reshape(1024, 256)) + dot_nt(
            left[:, 256:], wo_all[1].reshape(1024, 256)
        )

    copies, own = scatter_z(links, partial_of, send_buf, recv_buf)
    gathers = []
    for which, (weight, exponent, bits) in enumerate(
        ((w_gate, QEXP_MODEL, 4), (w_up, QEXP_MODEL, 4), (w_down, QEXP_HIDDEN, 2))
    ):
        wf_all[which, yh, yl * 2 + c] = quantized(weight[...], exponent, bits)
        gathers.append(Gather(links, wf_all, (which,)))
    branch = own
    for copy, slot in zip(copies, (1, 0, 2)):
        copy.wait_recv()
        branch = branch + recv_buf[slot].astype(F32)
    branch_out[...] = branch
    h1 = tokens[...].astype(F32) + branch * inverse_rms(branch) * gain_out[...]
    h1_out[...] = h1
    hn_all[z] = (h1 * inverse_rms(h1) * gain_in[...]).astype(BF16)
    ring = gather_z(links, hn_all)
    for gather in gathers:
        gather.forward()
    for copy in ring:
        copy.wait()
    for gather in gathers:
        gather.finish()
    for copy in copies:
        copy.wait_send()


def run_outproj(attn, wo_all, tokens, gain_out, gain_in, w_gate, w_up, w_down):
    return call(
        outproj_kernel, "outproj", 3,
        [
            ((128, 1024), F32), ((128, 1024), F32), ((4, 128, 1024), BF16),
            ((3, 2, 4, 256, 384), BF16),
        ],
        [VM] * 8, [pltpu.VMEM((3, 128, 1024), BF16)] * 2, 32,
    )(attn, wo_all, tokens, gain_out, gain_in, w_gate, w_up, w_down)


GELU_A = math.sqrt(2.0 / math.pi)
GELU_B = 0.044715


def gelu_parts(gate):
    square = gate * gate
    curve = jnp.tanh(GELU_A * gate * (1.0 + GELU_B * square))
    half = 0.5 * (1.0 + curve)
    slope = half + 0.5 * gate * (1.0 - curve * curve) * (
        GELU_A * (1.0 + 3.0 * GELU_B * square)
    )
    return gate * half, slope


def mlp_kernel(
    hn_all, wf_all, h1, gain_out, out_grad,
    gate_all, up_all, hidden_all, mixed_out, d_mlp_all, gain_grad,
    send_buf, recv_buf, send_sems, recv_sems,
):
    x, yh, z, yl, c = here()
    links = Links(send_sems, recv_sems)

    def partial_of(block):
        left = hn_all[block]
        total = None
        for group in range(2):
            cols = slice(group * 384, group * 384 + 384)
            gate = dot(left, wf_all[0, group].reshape(1024, 384))
            up = dot(left, wf_all[1, group].reshape(1024, 384))
            gate_all[block, :, cols] = gate
            up_all[block, :, cols] = up
            curve = jnp.tanh(GELU_A * gate * (1.0 + GELU_B * gate * gate))
            hidden = (0.5 * gate * (1.0 + curve) * up).astype(BF16)
            hidden_all[block, :, cols] = hidden
            term = dot_nt(hidden, wf_all[2, group].reshape(1024, 384))
            total = term if total is None else total + term
        return total

    greet([z_device(s) for s in (1, 2, 3)])
    copies, own = scatter_z(links, partial_of, send_buf, recv_buf)
    mlp = own
    for copy, slot in zip(copies, (1, 0, 2)):
        copy.wait_recv()
        mlp = mlp + recv_buf[slot].astype(F32)
    d_mlp, gain_part = rms_back(mlp, gain_out[...], out_grad[...].astype(F32))
    d_mlp_all[z] = d_mlp.astype(BF16)
    ring = gather_z(links, d_mlp_all)
    gain_grad[...] = gain_part
    mixed_out[...] = (h1[...] + mlp * inverse_rms(mlp) * gain_out[...]).astype(BF16)
    for copy in ring:
        copy.wait()
    for copy in copies:
        copy.wait_send()


def run_mlp(hn_all, wf_all, h1, gain_out, out_grad):
    return call(
        mlp_kernel, "mlp", 4,
        [
            ((4, 128, 768), F32), ((4, 128, 768), F32), ((4, 128, 768), BF16),
            ((128, 1024), BF16), ((4, 128, 1024), BF16), ((1, 1024), F32),
        ],
        [VM] * 5, [pltpu.VMEM((3, 128, 1024), BF16)] * 2, 8,
    )(hn_all, wf_all, h1, gain_out, out_grad)


class Shrink:
    def __init__(self, links, terms, pair_sum, middle, first_recv, last_recv, y_first):
        self.links = links
        self.terms = terms
        self.pair_sum = pair_sum
        self.middle = middle
        self.first_recv = first_recv
        self.last_recv = last_recv
        self.y_first = y_first
        self.copies = []

    def start(self):
        x, yh, z, yl, c = here()
        self.pair = self.links.send(self.terms.at[:, :, :, 1 - c], self.pair_sum, sibling())

    def send_first(self):
        x, yh, z, yl, c = here()
        self.pair.wait()
        terms, pair_sum = self.terms, self.pair_sum

        @pl.loop(0, 8)
        def _(at):
            h, k = lax.div(at, 4), lax.rem(at, 4)
            for low in range(2):
                pair_sum[h, k, low] = (
                    terms[h, k, low, c].astype(F32) + pair_sum[h, k, low].astype(F32)
                ).astype(BF16)

        self.first = []
        for step in (2, 1, 3):
            if self.y_first:
                device = y_device(step)
                source = pair_sum.at[device[1], :, device[3]]
            else:
                device = x_device(step)
                source = pair_sum.at[:, device[0]]
            self.first.append(self.links.send(source, self.first_recv.at[step - 1], device))

    def send_last(self):
        x, yh, z, yl, c = here()
        for copy in self.first:
            copy.wait()
        got = self.first_recv

        @pl.loop(0, 4)
        def _(at):
            if self.y_first:
                total = self.pair_sum[yh, at, yl].astype(F32)
                for slot in range(3):
                    total = total + got[slot, at].astype(F32)
                self.middle[at] = total.astype(BF16)
            else:
                h, low = lax.div(at, 2), lax.rem(at, 2)
                total = self.pair_sum[h, x, low].astype(F32)
                for slot in range(3):
                    total = total + got[slot, h, low].astype(F32)
                self.middle[h, low] = total.astype(BF16)

        self.second = []
        for step in (2, 1, 3):
            if self.y_first:
                device = x_device(step)
                source = self.middle.at[device[0]]
            else:
                device = y_device(step)
                source = self.middle.at[device[1], device[3]]
            self.second.append(self.links.send(source, self.last_recv.at[step - 1], device))

    def result(self):
        x, yh, z, yl, c = here()
        for copy in self.second:
            copy.wait()
        total = (self.middle[x] if self.y_first else self.middle[yh, yl]).astype(F32)
        for slot in range(3):
            total = total + self.last_recv[slot].astype(F32)
        return total


def shrink_scratch(rows, width, y_first):
    first = (4, rows, width) if y_first else (2, 2, rows, width)
    return [
        pltpu.VMEM((2, 4, 2, 2, rows, width), BF16),
        pltpu.VMEM((2, 4, 2, rows, width), BF16),
        pltpu.VMEM(first, BF16),
        pltpu.VMEM((3,) + first, BF16),
        pltpu.VMEM((3, rows, width), BF16),
    ]


def everyone():
    return (
        [z_device(s) for s in (1, 2, 3)]
        + [y_device(s) for s in (1, 2, 3)]
        + [x_device(s) for s in (1, 2, 3)]
        + [sibling()]
    )


def mlp_back_kernel(
    d_mlp_all, hidden_all, gate_all, up_all, wf_all, hn_all, h1, branch, out_grad, gain_in, gain_out,
    d_h1_out, d_branch_all, gain_in_grad, gain_out_grad, dwd_out, dwg_out, dwu_out,
    send_buf, recv_buf, d_gate_all, d_up_all,
    ta, pa, ma, fa, la, tb, pb, mb, fb, lb,
    send_sems, recv_sems,
):
    x, yh, z, yl, c = here()
    links = Links(send_sems, recv_sems)
    one = Shrink(links, ta, pa, ma, fa, la, True)
    two = Shrink(links, tb, pb, mb, fb, lb, False)

    def partial_of(block):
        left = d_mlp_all[block]
        total = None
        for group in range(2):
            cols = slice(group * 384, group * 384 + 384)
            d_hidden = dot(left, wf_all[2, group].reshape(1024, 384))
            value, slope = gelu_parts(gate_all[block, :, cols])
            d_gate = (d_hidden * up_all[block, :, cols] * slope).astype(BF16)
            d_up = (d_hidden * value).astype(BF16)
            d_gate_all[block, :, cols] = d_gate
            d_up_all[block, :, cols] = d_up
            term = dot_nt(d_gate, wf_all[0, group].reshape(1024, 384)) + dot_nt(
                d_up, wf_all[1, group].reshape(1024, 384)
            )
            total = term if total is None else total + term
        return total

    greet(everyone())
    copies, own = scatter_z(links, partial_of, send_buf, recv_buf)
    d_mlp = d_mlp_all[...].reshape(512, 1024)
    hn = hn_all[...].reshape(512, 1024)
    for group in range(2):
        cols = slice(group * 384, group * 384 + 384)
        down = dot_tn(d_mlp, hidden_all[:, :, cols].reshape(512, 384)).astype(BF16)
        ta[group, :, :, :, :, 0:384] = down.reshape(4, 2, 2, 64, 384)
        gate = dot_tn(hn, d_gate_all[:, :, cols].reshape(512, 384)).astype(BF16)
        gate = gate.reshape(4, 2, 2, 64, 384)
        ta[group, :, :, :, :, 384:640] = gate[..., 0:256]
        tb[group, :, :, :, :, 0:128] = gate[..., 256:384]
        up = dot_tn(hn, d_up_all[:, :, cols].reshape(512, 384)).astype(BF16)
        tb[group, :, :, :, :, 128:512] = up.reshape(4, 2, 2, 64, 384)
    one.start()
    two.start()
    d_hn = own
    for copy, slot in zip(copies, (1, 0, 2)):
        copy.wait_recv()
        d_hn = d_hn + recv_buf[slot].astype(F32)
    into, gain_part = rms_back(h1[...], gain_in[...], d_hn)
    gain_in_grad[...] = gain_part
    d_h1 = out_grad[...].astype(F32) + into
    d_h1_out[...] = d_h1
    into, gain_part = rms_back(branch[...], gain_out[...], d_h1)
    gain_out_grad[...] = gain_part
    d_branch_all[z] = into.astype(BF16)
    ring = gather_z(links, d_branch_all)
    one.send_first()
    two.send_first()
    one.send_last()
    two.send_last()
    first = one.result()
    dwd_out[...] = first[:, 0:384]
    dwg_out[:, 0:256] = first[:, 384:640]
    second = two.result()
    dwg_out[:, 256:384] = second[:, 0:128]
    dwu_out[...] = second[:, 128:512]
    for copy in ring:
        copy.wait()
    for copy in copies:
        copy.wait_send()


def run_mlp_back(d_mlp_all, hidden, gate, up, wf_all, hn_all, h1, branch, out_grad, gain_in, gain_out):
    return call(
        mlp_back_kernel, "mlp_back", 5,
        [
            ((128, 1024), F32), ((4, 128, 1024), BF16), ((1, 1024), F32), ((1, 1024), F32),
            ((64, 384), F32), ((64, 384), F32), ((64, 384), F32),
        ],
        [VM] * 11,
        [pltpu.VMEM((3, 128, 1024), BF16)] * 2
        + [pltpu.VMEM((4, 128, 768), BF16)] * 2
        + shrink_scratch(64, 640, True)
        + shrink_scratch(64, 512, False),
        24,
    )(d_mlp_all, hidden, gate, up, wf_all, hn_all, h1, branch, out_grad, gain_in, gain_out)


def attention_back_kernel(
    d_branch_all, wo_all, attn, recip, q, kv_all, cosd, sind, lengths,
    grads, dwo_out,
    d_out, d_q, d_kv, pair_recv, y_send, y_recv, total_kv,
    ta, pa, ma, fa, la, tb, pb, mb, fb, lb,
    send_sems, recv_sems,
):
    x, yh, z, yl, c = here()
    links = Links(send_sems, recv_sems)
    one = Shrink(links, ta, pa, ma, fa, la, True)
    two = Shrink(links, tb, pb, mb, fb, lb, False)
    greet(
        [y_device(s) for s in (1, 2, 3)] + [x_device(s) for s in (1, 2, 3)] + [sibling()]
    )
    d_branch = d_branch_all[...].reshape(512, 1024)
    for group in range(2):
        cols = slice(group * 256, group * 256 + 256)
        back = dot_tn(d_branch, attn[:, :, cols].reshape(512, 256)).astype(BF16)
        back = back.reshape(4, 2, 2, 64, 256)
        ta[group] = back[..., 0:128]
        tb[group] = back[..., 128:256]
    one.start()
    two.start()
    lane = lax.broadcasted_iota(jnp.int32, (256, 128), 1)
    for group in range(2):
        cols = slice(group * 256, group * 256 + 256)
        d_attn = dot(d_branch, wo_all[group].reshape(1024, 256)).astype(BF16)
        for block in range(4):
            rows = d_attn[block * 128 : block * 128 + 128].astype(F32)
            rows = jnp.concatenate([rows[:, :128], rows[:, 128:]], axis=0)
            outs = attn[block, :, cols].astype(F32)
            outs = jnp.concatenate([outs[:, :128], outs[:, 128:]], axis=0)
            scaled = (rows * recip[group, block]).astype(BF16)
            inner = -jnp.sum(scaled.astype(F32) * outs, axis=1, keepdims=True)
            high = inner.astype(BF16)
            low = (inner - high.astype(F32)).astype(BF16)
            extra = jnp.where(
                lane == 0, high.astype(F32), jnp.where(lane == 1, low.astype(F32), 0.0)
            )
            d_out[group, block] = jnp.concatenate([scaled, extra.astype(BF16)], axis=1)
    d_q[...] = jnp.zeros_like(d_q)
    start = lengths[0, 0]
    ones = jnp.where(lane < 2, 1.0, 0.0).astype(BF16)
    token_row = lax.broadcasted_iota(jnp.int32, (1, 256), 1)

    def unit_back(group, from_h, from_l, unit, first_block):
        both = kv_all[group, from_h, from_l, unit].reshape(256, 256)
        key, value = both[:, :128], both[:, 128:]
        count = 4 - first_block
        query = q[group, first_block:].reshape(count * 256, 128)
        cot = d_out[group, first_block:].reshape(count * 256, 256)
        curved = jnp.tanh(dot_nt(key, query) * (1.0 / CAP))
        weight = jnp.exp(curved * CAP)
        base = yh * 2048 + yl * 256 + c * 128
        token_q = jnp.concatenate(
            [
                base + block * 512 + lax.rem(token_row, 128)
                for block in range(first_block, 4)
            ],
            axis=1,
        )
        floor = jnp.where(token_q >= start, start, 0)
        key_base = from_h * 2048 + unit * 512 + from_l * 256
        token_k = key_base + lax.broadcasted_iota(jnp.int32, (256, 1), 0)
        seen = (token_k >= floor) & (token_k <= token_q)
        weight = jnp.where(seen, weight, 0.0)
        grown = dot_nt(jnp.concatenate([value, ones], axis=1), cot)
        slope = (weight * grown * (1.0 - curved * curved)).astype(BF16)
        d_key = dot(slope, query)
        d_value = dot(weight.astype(BF16), cot[:, :128])
        d_kv[group, from_h, from_l, unit] = (
            jnp.concatenate([d_key, d_value], axis=1).astype(BF16).reshape(2, 128, 256)
        )
        d_q[group, :, first_block * 256 :] += dot(key.T, slope)

    def same_half(from_l):
        @pl.loop(0, 2)
        def _(group):
            for unit in range(4):
                unit_back(group, yh, from_l, unit, unit)

    def other_half(from_l):
        @pl.loop(0, 8)
        def _(at):
            unit_back(lax.div(at, 4), 0, from_l, lax.rem(at, 4), 0)

    def pair_plan(slot, from_h, from_l):
        return links.plan(
            d_kv.at[:, from_h, from_l, :, 1 - c], pair_recv.at[slot], sibling()
        )

    def add_pair(slot, from_h, from_l):
        return d_kv[:, from_h, from_l, :, c].astype(F32) + pair_recv[slot].astype(F32)

    far_pair = [pair_plan(0, 0, 1 - yl), pair_plan(1, 0, yl)]
    far_send = [
        links.plan(y_send.at[0], y_recv.at[0], (x, 0, z, 1 - yl, c)),
        links.plan(y_send.at[1], y_recv.at[1], (x, 0, z, yl, c)),
    ]

    @pl.when(yh == 1)
    def _():
        other_half(1 - yl)
        far_pair[0].start()
        other_half(yl)
        far_pair[1].start()
        far_pair[0].wait()
        y_send[0] = add_pair(0, 0, 1 - yl).astype(BF16)
        far_send[0].start()

    one.send_first()
    two.send_first()
    same_half(1 - yl)
    near_pair = pair_plan(2, yh, 1 - yl)
    near_pair.start()

    @pl.when(yh == 1)
    def _():
        far_pair[1].wait()
        y_send[1] = add_pair(1, 0, yl).astype(BF16)
        far_send[1].start()

    near_pair.wait()
    y_send[2] = add_pair(2, yh, 1 - yl).astype(BF16)
    near_send = links.send(y_send.at[2], y_recv.at[2], (x, yh, z, 1 - yl, c))
    one.send_last()
    two.send_last()
    same_half(yl)
    own_pair = pair_plan(3, yh, yl)
    own_pair.start()
    cos_rows = cosd[...]
    sin_rows = sind[...]

    def rope_back(values, block):
        return values * cos_rows[block] - swap_halves(values) * sin_rows[block]

    for group in range(2):
        d_query = d_q[group].T
        for block in range(4):
            for head in range(2):
                first = block * 256 + head * 128
                turned = rope_back(d_query[first : first + 128], block) * SCALE
                at = group * 256 + head * 128
                grads[block, :, at : at + 128] = turned.astype(BF16)
    dwo_out[:, 0:128] = one.result()
    dwo_out[:, 128:256] = two.result()
    own_pair.wait()
    total_kv[...] = add_pair(3, yh, yl)
    near_send.wait()
    total_kv[...] += y_recv[2].astype(F32)

    @pl.when(yh == 0)
    def _():
        for slot in range(2):
            far_send[slot].wait_recv()
            total_kv[...] += y_recv[slot].astype(F32)

    @pl.when(yh == 1)
    def _():
        for slot in range(2):
            far_send[slot].wait_send()

    for group in range(2):
        for block in range(4):
            both = total_kv[group, block]
            d_key = both[:, :128].astype(BF16).astype(F32)
            at = 512 + group * 128
            grads[block, :, at : at + 128] = rope_back(d_key, block).astype(BF16)
            at = 768 + group * 128
            grads[block, :, at : at + 128] = both[:, 128:].astype(BF16)


def run_attention_back(d_branch_all, wo_all, attn, recip, q, kv_all, cosd, sind, lengths):
    return call(
        attention_back_kernel, "attention_back", 6,
        [((4, 128, 1024), BF16), ((64, 256), F32)],
        [VM] * 8 + [SM],
        [
            pltpu.VMEM((2, 4, 256, 256), BF16),
            pltpu.VMEM((2, 128, 1024), F32),
            pltpu.VMEM((2, 2, 2, 4, 2, 128, 256), BF16),
            pltpu.VMEM((4, 2, 4, 128, 256), BF16),
            pltpu.VMEM((3, 2, 4, 128, 256), BF16),
            pltpu.VMEM((3, 2, 4, 128, 256), BF16),
            pltpu.VMEM((2, 4, 128, 256), F32),
        ]
        + shrink_scratch(64, 128, True)
        + shrink_scratch(64, 128, False),
        24,
    )(d_branch_all, wo_all, attn, recip, q, kv_all, cosd, sind, lengths)


def input_back_kernel(
    grads, wq_all, wkv_all, xn_all, tokens, gain, d_h1, gain_two, gain_three, gain_four,
    tokens_grad, dwq_out, dwk_out, dwv_out, gain_sums,
    send_buf, recv_buf, folded, kv_send, kv_recv, gain_own, gain_pair, gain_y, gain_x, gain_z,
    ta, pa, ma, fa, la, tb, pb, mb, fb, lb,
    send_sems, recv_sems,
):
    x, yh, z, yl, c = here()
    links = Links(send_sems, recv_sems)
    one = Shrink(links, ta, pa, ma, fa, la, True)
    two = Shrink(links, tb, pb, mb, fb, lb, False)
    gain_own[...] = jnp.zeros_like(gain_own)

    def partial_of(block):
        left = grads[block]
        total = dot_nt(left[:, 512:], wkv_all[...].reshape(1024, 512))
        for group in range(2):
            total = total + dot_nt(
                left[:, group * 256 : group * 256 + 256], wq_all[group].reshape(1024, 256)
            )
        gain_own[0:1] += jnp.sum(total * xn_all[block].astype(F32), axis=0, keepdims=True)
        return total

    greet(everyone())
    copies, own = scatter_z(links, partial_of, send_buf, recv_buf)
    gain_own[0:1] = gain_own[0:1] / gain[...]
    gain_own[1:2] = gain_two[...]
    gain_own[2:3] = gain_three[...]
    gain_own[3:4] = gain_four[...]
    pair = links.send(gain_own, gain_pair, sibling())
    xa = xn_all[...].reshape(512, 1024)
    for group in range(2):
        back = dot_tn(xa, grads[:, :, group * 256 : group * 256 + 256].reshape(512, 256))
        ta[group] = back.astype(BF16).reshape(4, 2, 2, 64, 256)
    one.start()
    back = dot_tn(xa, grads[:, :, 512:].reshape(512, 512))
    for k in range(4):
        for h in range(2):
            for block in range(4):
                first = k * 256 + h * 128 + block * 32
                folded[k, h, :, :, block] = back[first : first + 32].reshape(2, 2, 8, 512)
    for h in range(2):
        for k in range(4):
            for low in range(2):
                tb[h, k, low] = folded[k, h, low].reshape(2, 32, 512).astype(BF16)
    two.start()
    pair.wait()
    gain_pair[...] += gain_own[...]
    sent = [links.send(gain_pair, gain_y.at[s - 1], y_device(s)) for s in (2, 1, 3)]
    one.send_first()
    two.send_first()
    for copy in sent:
        copy.wait()
    total = gain_pair[...]
    gain_own[...] = total + (gain_y[0] + gain_y[2]) + gain_y[1]
    sent = [links.send(gain_own, gain_x.at[s - 1], x_device(s)) for s in (2, 1, 3)]
    d_xn = own
    for copy, slot in zip(copies, (1, 0, 2)):
        copy.wait_recv()
        d_xn = d_xn + recv_buf[slot].astype(F32)
    into, _ = rms_back(tokens[...].astype(F32), gain[...], d_xn)
    tokens_grad[...] = (d_h1[...] + into).astype(BF16)
    for copy in sent:
        copy.wait()
    gain_pair[...] = gain_own[...] + (gain_x[0] + gain_x[2]) + gain_x[1]
    sent = [links.send(gain_pair, gain_z.at[s - 1], z_device(s)) for s in (2, 1, 3)]
    one.send_last()
    two.send_last()
    dwq_out[...] = one.result()
    kv_send[...] = two.result().reshape(4, 8, 512)
    moved = []
    for s in (2, 1, 3):
        device = z_device(s)
        moved.append(links.send(kv_send.at[device[2]], kv_recv.at[z], device))
    kv_recv[z] = kv_send[z]
    for copy in sent:
        copy.wait()
    gain_sums[...] = gain_pair[...] + (gain_z[0] + gain_z[2]) + gain_z[1]
    for copy in moved:
        copy.wait()
    for origin in range(4):
        for group in range(2):
            at = group * 512 + origin * 128
            dwk_out[:, at : at + 128] = kv_recv[origin, :, group * 128 : group * 128 + 128]
            dwv_out[:, at : at + 128] = kv_recv[
                origin, :, 256 + group * 128 : 384 + group * 128
            ]
    for copy in copies:
        copy.wait_send()


def run_input_back(
    grads, wq_all, wkv_all, xn_all, tokens, gain, d_h1, gain_two, gain_three, gain_four
):
    return call(
        input_back_kernel, "input_back", 7,
        [
            ((128, 1024), BF16), ((64, 256), F32), ((8, 1024), F32), ((8, 1024), F32),
            ((8, 1024), F32),
        ],
        [VM] * 10,
        [pltpu.VMEM((3, 128, 1024), BF16)] * 2
        + [
            pltpu.VMEM((4, 2, 2, 2, 4, 8, 512), F32),
            pltpu.VMEM((4, 8, 512), F32),
            pltpu.VMEM((4, 8, 512), F32),
            pltpu.VMEM((8, 1024), F32),
            pltpu.VMEM((8, 1024), F32),
            pltpu.VMEM((3, 8, 1024), F32),
            pltpu.VMEM((3, 8, 1024), F32),
            pltpu.VMEM((3, 8, 1024), F32),
        ]
        + shrink_scratch(64, 256, True)
        + shrink_scratch(32, 512, False),
        32,
    )(grads, wq_all, wkv_all, xn_all, tokens, gain, d_h1, gain_two, gain_three, gain_four)


def per_device(
    tokens, lengths, w_query, w_key, w_value, w_output, w_gate, w_up, w_down,
    gain_attn_in, gain_attn_out, gain_mlp_in, gain_mlp_out, out_grad,
):
    gain_attn_in, gain_attn_out, gain_mlp_in, gain_mlp_out = (
        gain.reshape(1, -1) for gain in (gain_attn_in, gain_attn_out, gain_mlp_in, gain_mlp_out)
    )
    xn_all, wq_all, wkv_all, q, kv, cosd, sind = run_qkv(
        tokens, gain_attn_in, w_query, w_key, w_value, lengths
    )
    kv_all, attn, recip, wo_all = run_attention(q, kv, w_output, lengths)
    branch, h1, hn_all, wf_all = run_outproj(
        attn, wo_all, tokens, gain_attn_out, gain_mlp_in, w_gate, w_up, w_down
    )
    gate, up, hidden, mixed, d_mlp_all, gain_four = run_mlp(
        hn_all, wf_all, h1, gain_mlp_out, out_grad
    )
    d_h1, d_branch_all, gain_three, gain_two, dwd, dwg, dwu = run_mlp_back(
        d_mlp_all, hidden, gate, up, wf_all, hn_all, h1, branch, out_grad,
        gain_mlp_in, gain_attn_out,
    )
    grads, dwo = run_attention_back(
        d_branch_all, wo_all, attn, recip, q, kv_all, cosd, sind, lengths
    )
    tokens_grad, dwq, dwk, dwv, gains = run_input_back(
        grads, wq_all, wkv_all, xn_all, tokens, gain_attn_in, d_h1,
        gain_two, gain_three, gain_four,
    )
    x, yh, z, yl, c = here()
    first = ((((x * 2 + yh) * 4 + z) * 2 + yl) * 2 + c) * 8
    own_gains = lax.dynamic_slice(gains, (0, first), (4, 8))
    return (
        mixed, tokens_grad, dwq, dwk, dwv, dwo, dwg, dwu, dwd,
        own_gains[0], own_gains[1], own_gains[2], own_gains[3],
    )


def solution(mesh):
    grid = Mesh(mesh.devices.reshape(4, 2, 4, 2, 2), AXES)
    tokens = P(AXES, None)
    split = P(("yl", "c"), ("yh", "z"))
    rows = P(("yl", "c"), None)
    grads = P(("x", "yl", "c"), ("yh", "z"))
    gains = P(AXES)
    return jax.shard_map(
        per_device,
        mesh=grid,
        in_specs=(tokens, P("x", None), split, rows, rows, split, split, split, split)
        + (P(),) * 4
        + (tokens,),
        out_specs=(tokens, tokens, grads, tokens, tokens, grads, grads, grads, grads)
        + (gains,) * 4,
        check_vma=False,
    )
```

time: 2140 us -> 305 us (0.14)
  waiting for transfers between devices: 1730 us -> 0 us
  Pallas kernels: 0 us -> 288 us
  matrix products: 151 us -> 0 us
  blocking collectives: 121 us -> 0 us
  other arithmetic: 82.8 us -> 0 us
    reduce_scatter x7 -> x0, waiting for transfers between devices: 1510 us -> none  [the longest x1 641 us: per_device(): lax.psum_scatter(key_full, ('seq', 'head', 'rows'), scatter_dimension=0,...]
    pallas_call x0 -> x7, Pallas kernels: none -> 288 us  [the longest x1 61.8 us: run_attention_back(): call(attention_back_kernel, 'attention_back', 6, [((4, 128, 1024), BF16),...]
    all_gather x6 -> x0, waiting for transfers between devices: 166 us -> none  [the longest x4 157 us: gather_heads(): return lax.all_gather(values, 'head', axis=0, tiled=True)]
    dot_general x22 -> x0, matrix products: 151 us -> none  [the longest x1 27.2 us: per_device(): jnp.einsum('upfa,ypa->pfuy', attended_layout, backward_values_layout, pre...]
    unnamed x1 -> x0, blocking collectives: 64.9 us -> none
    all_gather x7 -> x0, blocking collectives: 55.7 us -> none  [the longest x1 11.5 us: per_device(): lax.all_gather(w_up, 'rows', axis=0, tiled=True)]
    unnamed x15 -> x0, waiting for transfers between devices: 51.7 us -> none
    another operation x5 -> x0, other arithmetic: 32.4 us -> none
  transfers between devices with their start and end apart: 14 -> 0, of which waited for: 12 -> 0; matrix products, arithmetic and copies ran while one was open for 5% -> 0% of each run, Pallas kernels for 0% -> 0%
where the time goes in v2:
time: 305 us; the launch traced here: 299 us
  Pallas kernels  288 us (94%)
  local copies, waits for them, and re-layouts  10.4 us (3%)
    pallas_call x1, Pallas kernels, run_attention_back(): call(attention_back_kernel, 'attention_back', 6, [((4, 128, 1024), BF16),...  61.8 us
    pallas_call x1, Pallas kernels, run_outproj(): call(outproj_kernel, 'outproj', 3, [((128, 1024), F32), ((128, 1024), F32...  51.1 us
    pallas_call x1, Pallas kernels, run_mlp_back(): call(mlp_back_kernel, 'mlp_back', 5, [((128, 1024), F32), ((4, 128, 1024)...  47.1 us
    pallas_call x1, Pallas kernels, run_attention(): call(attention_kernel, 'attention', 2, [((2, 2, 2, 4, 2, 128, 256), BF16)...  36.8 us
    pallas_call x1, Pallas kernels, run_mlp(): call(mlp_kernel, 'mlp', 4, [((4, 128, 768), F32), ((4, 128, 768), F32), (...  36.2 us
    pallas_call x1, Pallas kernels, run_input_back(): call(input_back_kernel, 'input_back', 7, [((128, 1024), BF16), ((64, 256)...  30.1 us
    pallas_call x1, Pallas kernels, run_qkv(): call(qkv_kernel, 'qkv', 1, [((4, 128, 1024), BF16), ((2, 4, 256, 256), BF...  24.8 us
    unnamed x19, local copies, waits for them, and re-layouts  9.16 us

profile of v2, /device:TPU:0, one launch (start us, length us, event | category | flops | bytes accessed | tf_op | source)
XLA Modules:
  0.0 299.5 jit_solution(949552012528295464)
XLA Ops:
  0.6 24.8 %qkv.1 = (bf16[4,128,1024]{2,1,0:T(8,128)(2,1)}, bf16[2,4,256,256]{3,2,1,0:T(8,128)(2,1)}, bf16[4,256,512]{2,1,0:T(8,128)(2,1)}, bf16[2,4,2,128,128]{4,3,2,1,0:T...) custom-call(bf16[128,1024]{1,0:T(8,128)(2,1)} %tokens.5, ...), custom_call_target="tpu_custom_call" | custom-call | tf_op jit(solution)/shard_map/qkv/pallas_call | solution.py:238
  25.4 36.8 %attention.1 = (bf16[2,2,2,4,2,128,256]{6,5,4,3,2,1,0:T(8,128)(2,1)}, bf16[4,128,512]{2,1,0:T(8,128)(2,1)}, f32[2,4,256,128]{3,2,1,0:T(8,128)}, bf16[2,4,256,256]{3,2,1,0:T(8,128)(2,1)}) custom-call(bf16[2,4,2,128,128]{4,3,2,1,0:T(8,128)(2,1)} %get-tuple-element.48.q, bf16[2,4,128,256]{3,2,1,0:T(8,128)(2,1)} %get-tuple-element.49.kv, ...), custom_call_target="tpu_custom_call" | custom-call | tf_op jit(solution)/shard_map/attention/pallas_call | solution.py:366
  62.2 51.1 %outproj.1 = (f32[128,1024]{1,0:T(8,128)}, f32[128,1024]{1,0:T(8,128)}, bf16[4,128,1024]{2,1,0:T(8,128)(2,1)}, bf16[3,2,4,256,384]{4,3,2,1,0:T(8,128)(2,1)}) custom-call(bf16[4,128,512]{2,1,0:T(8,128)(2,1)} %get-tuple-element.50.attn, bf16[2,4,256,256]{3,2,1,0:T(8,128)(2,1)} %get-tuple-element.51.wo_all, bf16[128,1024]{1,0:T(8,128)(2,1)} %tokens.5, ...), custom_call_target="tpu_custom_call" | custom-call | tf_op jit(solution)/shard_map/outproj/pallas_call | solution.py:432
  113.3 36.2 %mlp.1 = (f32[4,128,768]{2,1,0:T(8,128)}, f32[4,128,768]{2,1,0:T(8,128)}, bf16[4,128,768]{2,1,0:T(8,128)(2,1)}, bf16[128,1024]{1,0:T(8,128)(2,1)}, bf16[4,128,1024]{2,1,0:T(8,128)(2,1)}, /*index=5*/f32[1,1024]{1,0:T(1,128)}) custom-call(bf16[4,128,1024]{2,1,0:T(8,128)(2,1)} %get-tuple-element.52.hn_all, ...), custom_call_target="tpu_custom_call" | custom-call | tf_op jit(solution)/shard_map/mlp/pallas_call | solution.py:498
  149.5 47.1 %mlp_back.1 = (f32[128,1024]{1,0:T(8,128)}, bf16[4,128,1024]{2,1,0:T(8,128)(2,1)}, f32[1,1024]{1,0:T(1,128)}, f32[1,1024]{1,0:T(1,128)}, f32[64,384]{1,0:T(8,128...) custom-call(bf16[4,128,1024]{2,1,0:T(8,128)(2,1)} %get-tuple-element.56.d_mlp_all, ...), custom_call_target="tpu_custom_call" | custom-call | tf_op jit(solution)/shard_map/mlp_back/pallas_call | solution.py:680
  196.6 61.8 %attention_back.1 = (bf16[4,128,1024]{2,1,0:T(8,128)(2,1)}, f32[64,256]{1,0:T(8,128)}) custom-call(bf16[4,128,1024]{2,1,0:T(8,128)(2,1)} %get-tuple-element.61.d_branch_all, bf16[2,4,256,256]{3,2,1,0:T(8,128)(2,1)} %get-tuple-element.51.wo_all, bf16[4,128,512]{2,1,0:T(8,128)(2,1)} %get-tuple-element.50.attn, f32[2,4,256,128]{3,2,1,0:T(8,128)} %get-tuple-element.62.recip, ...), custom_call_target="tpu_custom_call" | custom-call | tf_op jit(solution)/shard_map/attention_back/pallas_call | solution.py:868
  258.4 0.0 copy-start
  258.4 0.0 copy-start.4
  258.4 0.0 copy-start.3
  258.4 0.0 copy-start.2
  258.5 0.0 copy-start.1
  258.5 30.1 %input_back.1 = (bf16[128,1024]{1,0:T(8,128)(2,1)}, f32[64,256]{1,0:T(8,128)}, f32[8,1024]{1,0:T(8,128)}, f32[8,1024]{1,0:T(8,128)}, f32[8,1024]{1,0:T(8,128)}) custom-call(bf16[4,128,1024]{2,1,0:T(8,128)(2,1)} %get-tuple-element.66.grads, bf16[2,4,256,256]{3,2,1,0:T(8,128)(2,1)} %get-tuple-element.67.wq_all, ...), custom_call_target="tpu_custom_call" | custom-call | tf_op jit(solution)/shard_map/input_back/pallas_call | solution.py:981
  288.6 0.7 constant_dynamic-slice_fusion
  289.4 0.5 slice_bitcast_fusion
  289.9 0.0 copy-done
  289.9 0.7 copy.36
  290.6 1.7 copy.37
  292.3 1.5 copy.38
  293.7 1.4 copy.39
  295.1 1.4 copy.40
  296.5 0.0 copy-done.4
  296.5 0.6 copy.41
  297.1 0.0 copy-done.3
  297.1 0.6 copy.42
  297.8 0.0 copy-done.2
  297.8 0.6 copy.43
  298.4 0.0 copy-done.1
  298.4 0.6 copy.44
Async XLA Ops:
  258.4 31.5 %copy-start = (bf16[128,1024]{1,0:T(8,128)(2,1)S(1)}, bf16[128,1024]{1,0:T(8,128)(2,1)}, u32[]{:S(2)}) copy-start(bf16[128,1024]{1,0:T(8,128)(2,1)} %get-tuple-element.100) | copy-start | bytes 786436
  258.4 38.1 %copy-start.4 = (f32[64,256]{1,0:T(8,128)S(1)}, f32[64,256]{1,0:T(8,128)}, u32[]{:S(2)}) copy-start(f32[64,256]{1,0:T(8,128)} %get-tuple-element.105) | copy-start | bytes 196612
  258.4 38.7 %copy-start.3 = (f32[64,384]{1,0:T(8,128)S(1)}, f32[64,384]{1,0:T(8,128)}, u32[]{:S(2)}) copy-start(f32[64,384]{1,0:T(8,128)} %get-tuple-element.106) | copy-start | bytes 294916
  258.4 39.3 %copy-start.2 = (f32[64,384]{1,0:T(8,128)S(1)}, f32[64,384]{1,0:T(8,128)}, u32[]{:S(2)}) copy-start(f32[64,384]{1,0:T(8,128)} %get-tuple-element.107) | copy-start | bytes 294916
  258.5 39.9 %copy-start.1 = (f32[64,384]{1,0:T(8,128)S(1)}, f32[64,384]{1,0:T(8,128)}, u32[]{:S(2)}) copy-start(f32[64,384]{1,0:T(8,128)} %get-tuple-element.108) | copy-start | bytes 294916
